TPU v7x, 32 devices: a whole 2x2x4 slice. The times are simulated.
32 devices in a mesh: filt: 2 (over core), row: 4 (over y, x), col: 4 (over z).
Axes of the slice: x: 2, y: 2, z: 4, core: 2. Of those that a mesh axis runs over, the one named last changes fastest.
Arguments:
- particles: bfloat16 [3072, 256], P(('filt', 'row', 'col')), parts along dimension 0, may hold values from -6 to 6
- cotangent: bfloat16 [3072, 256], P(('filt', 'row', 'col')), parts along dimension 0, may hold values from -3 to 3
- row_potential: bfloat16 [3072], P(('filt', 'row', 'col')), parts along dimension 0, may hold values from -0.099609375 to 0.099609375
- col_potential: bfloat16 [3072], P(('filt', 'row', 'col')), parts along dimension 0, may hold values from -0.099609375 to 0.099609375
- weights: bfloat16 [3072], P(('filt', 'row', 'col')), parts along dimension 0, may hold values from 0.5 to 18
Outputs:
- grad_particles: bfloat16 [3072, 256], P(('filt', 'row', 'col')), parts along dimension 0
- grad_weights: float32 [3072], P(('filt', 'row', 'col')), parts along dimension 0
There are 2 independent parts, one for each index of `filt`. A program takes and returns all parts, laid end to end along the dimension named above; each array names one. Nothing has to cross between parts.
All inputs are finite; a program needn't handle non-finite values.
Results may differ from a plain program's by a relative error of at most 0.02.
Values may be sent and summed in bfloat16 or wider, within the bound.
A program may use at most 64 MiB of HBM per device.

v0:
```python
import jax
import jax.numpy as jnp
from jax import lax
from jax.sharding import PartitionSpec as P

ITERS = 4


EPS = 0.09


def local(particles, cotangent, row_potential, col_potential, weights):
    row_parts, row_fpot, row_wts = (
        lax.all_gather(particles, "col", axis=0, tiled=True),
        lax.all_gather(row_potential, "col", axis=0, tiled=True),
        lax.all_gather(weights, "col", axis=0, tiled=True),
    )
    col_parts, col_grads, col_gpot = (
        lax.all_gather(particles, "row", axis=0, tiled=True),
        lax.all_gather(cotangent, "row", axis=0, tiled=True),
        lax.all_gather(col_potential, "row", axis=0, tiled=True),
    )
    own = particles.shape[0]
    width = particles.shape[1]
    rows = row_parts.shape[0]
    cols = col_parts.shape[0]
    blk = 512 if rows % 512 == 0 else rows
    count = rows // blk
    row_float = row_parts.astype(jnp.float32)
    row_sq = jnp.sum(row_float * row_float, axis=1)
    col_float = col_parts.astype(jnp.float32)
    col_sq = jnp.sum(col_float * col_float, axis=1)
    fpot = row_fpot.astype(jnp.float32)
    gpot = col_gpot.astype(jnp.float32)
    stacked = jnp.concatenate([col_parts, col_grads], axis=0)
    items = (
        row_parts.reshape(count, blk, width),
        fpot.reshape(count, blk),
        row_sq.reshape(count, blk),
    )

    def plan_from(cross, pot_blk, sq_blk):
        cost = (sq_blk[:, None] + col_sq[None, :] - 2.0 * cross) / (2.0 * width)
        return jnp.exp((pot_blk[:, None] + gpot[None, :] - cost) / EPS)

    def plan_only(part_blk, pot_blk, sq_blk):
        cross = jnp.einsum("rd,cd->rc", part_blk, col_parts, preferred_element_type=jnp.float32)
        return plan_from(cross, pot_blk, sq_blk)

    def first(carry, item):
        part_blk, pot_blk, sq_blk = item
        both = jnp.einsum("rd,cd->rc", part_blk, stacked, preferred_element_type=jnp.float32)
        plan = plan_from(both[:, :cols], pot_blk, sq_blk)
        weighted = plan * both[:, cols:]
        return (
            (carry[0] + jnp.sum(plan, axis=0), carry[1] + jnp.sum(weighted, axis=0)),
            (jnp.sum(plan, axis=1), jnp.sum(weighted, axis=1)),
        )

    zeros_c = jnp.zeros((cols,), jnp.float32)
    (colmass_part, colph_part), (rowmass_part, rowph_part) = lax.scan(
        first, (zeros_c, zeros_c), items
    )
    rowmass, rowph = lax.psum((rowmass_part.reshape(rows), rowph_part.reshape(rows)), "col")
    colmass, colph = lax.psum((colmass_part, colph_part), "row")
    psi = zeros_c
    phi = jnp.zeros((rows,), jnp.float32)
    for step in range(ITERS):

        def apply_rows(carry, item):
            plan = plan_only(item[0], item[1], item[2])
            return (carry, jnp.dot(plan, psi, precision=lax.Precision.HIGHEST))

        unused, row_apply = lax.scan(apply_rows, jnp.zeros((), jnp.float32), items)
        row_total = lax.psum(row_apply.reshape(rows), "col")
        phi = -(rowph + row_total) / rowmass

        def apply_cols(acc, item):
            plan = plan_only(item[0], item[1], item[2])
            return (acc + jnp.dot(item[3], plan, precision=lax.Precision.HIGHEST), None)

        col_apply, unused_out = lax.scan(apply_cols, zeros_c, items + (phi.reshape(count, blk),))
        col_total = lax.psum(col_apply, "row")
        psi = -(colph + col_total) / colmass

    def last(acc, item):
        part_blk, pot_blk, sq_blk, phi_blk = item
        both = jnp.einsum("rd,cd->rc", part_blk, stacked, preferred_element_type=jnp.float32)
        plan = plan_from(both[:, :cols], pot_blk, sq_blk)
        mixed = plan * (both[:, cols:] + phi_blk[:, None] + psi[None, :])
        qrow = jnp.sum(mixed, axis=1)
        plan_bf = plan.astype(jnp.bfloat16)
        mixed_bf = mixed.astype(jnp.bfloat16)
        rowterm = jnp.dot(plan_bf, col_grads, preferred_element_type=jnp.float32)
        rowterm = rowterm + (
            jnp.dot(mixed_bf, col_parts, preferred_element_type=jnp.float32)
            - qrow[:, None] * part_blk.astype(jnp.float32)
        ) / (width * EPS)
        return (
            acc + jnp.einsum("rc,rd->cd", mixed_bf, part_blk, preferred_element_type=jnp.float32),
            rowterm,
        )

    col_acc, row_terms = lax.scan(
        last, jnp.zeros((cols, width), jnp.float32), items + (phi.reshape(count, blk),)
    )
    row_terms = row_terms.reshape(rows, width)
    start = lax.axis_index("col") * own
    summed = lax.psum(row_terms.astype(jnp.bfloat16), "col").astype(jnp.float32)
    row_own = lax.dynamic_slice_in_dim(summed, start, own, 0)
    col_own = lax.psum_scatter(
        col_acc.astype(jnp.bfloat16), "row", scatter_dimension=0, tiled=True
    ).astype(jnp.float32)
    grad_particles = (row_own + col_own / (width * EPS)).astype(jnp.bfloat16)
    phi_own = lax.dynamic_slice_in_dim(phi, start, own, 0)
    own_wts = weights.astype(jnp.float32)
    total, wphi = lax.psum((jnp.sum(own_wts), jnp.sum(own_wts * phi_own)), ("row", "col"))
    count_all = rows * lax.axis_size("row")
    grad_weights = -(count_all / total) * (phi_own - wphi / total)
    return (grad_particles, grad_weights)


def solution(mesh):
    return jax.shard_map(
        local,
        mesh=mesh,
        in_specs=(
            P(("filt", "row", "col"), None),
            P(("filt", "row", "col"), None),
            P(("filt", "row", "col")),
            P(("filt", "row", "col")),
            P(("filt", "row", "col")),
        ),
        out_specs=(P(("filt", "row", "col"), None), P(("filt", "row", "col"))),
        check_vma=False,
    )
```

profile of v0, /device:TPU:0, one launch (start us, length us, event | category | flops | bytes accessed | tf_op | source)
XLA Modules:
  0.0 196.1 jit_solution(2865896469630730700)
XLA Ops:
  8.0 0.0 all-reduce.7.cloned.1.call-start
  8.0 15.7 %all_gather.17 = bf16[384,256]{1,0:T(8,128)(2,1)S(1)} all-gather(bf16[96,256]{1,0:T(8,128)(2,1)} %param.5), channel_id=1, replica_groups=mesh['filt'=2,'row'=4,'col'=4] {'col'}, dimensions={0}, use_global_device_ids=true | all-gather | bytes 245760 | tf_op jit(solution)/shard_map/all_gather | solution.py:14
  23.7 9.0 %all_gather.18 = bf16[384,256]{1,0:T(8,128)(2,1)S(1)} all-gather(bf16[96,256]{1,0:T(8,128)(2,1)} %param.5), channel_id=1, replica_groups=mesh['filt'=2,'row'=4,'col'=4] {'row'}, dimensions={0}, use_global_device_ids=true | all-gather | bytes 245760 | tf_op jit(solution)/shard_map/all_gather | solution.py:19
  32.7 0.0 copy-start.3
  32.7 0.0 copy-start.2
  32.7 8.6 %all_gather.19 = bf16[384,256]{1,0:T(8,128)(2,1)S(1)} all-gather(bf16[96,256]{1,0:T(8,128)(2,1)} %param.6), channel_id=1, replica_groups=mesh['filt'=2,'row'=4,'col'=4] {'row'}, dimensions={0}, use_global_device_ids=true | all-gather | bytes 245760 | tf_op jit(solution)/shard_map/all_gather | solution.py:20
  41.3 0.1 multiply_reduce_fusion
  41.5 0.2 fusion.10
  41.6 0.4 convolution_bitcast_fusion
  42.0 0.0 copy-done.4
  42.0 0.6 dynamic-slice.8
  43.3 0.0 copy-done.1
  43.3 0.2 dynamic-update-slice.1
  43.5 8.9 %all-reduce.1 = bf16[384]{0:T(512)(128)(2,1)S(1)} all-reduce(bf16[384]{0:T(512)(128)(2,1)S(1)} %dynamic-update-slice.1), channel_id=1, replica_groups=mesh['filt'=2,'row'=4,'col'=4] {'row'}, use_global_device_ids=true, to_apply=%add.1 | all-reduce | flops 384 | bytes 1536
  52.4 0.6 dynamic-slice.7
  53.7 0.2 dynamic-update-slice
  53.9 12.0 %all-reduce = bf16[384]{0:T(512)(128)(2,1)S(1)} all-reduce(bf16[384]{0:T(512)(128)(2,1)S(1)} %dynamic-update-slice), channel_id=1, replica_groups=mesh['filt'=2,'row'=4,'col'=4] {'col'}, use_global_device_ids=true, to_apply=%add | all-reduce | flops 384 | bytes 1536
  66.0 0.3 fusion.4
  66.3 0.4 fusion.16
  66.7 0.5 convolution_reduce_fusion.7
  67.2 8.5 %all-reduce.3 = (f32[384]{0:T(512)S(1)}, f32[384]{0:T(512)S(1)}, f32[384]{0:T(512)S(1)}) all-reduce(f32[384]{0:T(512)S(1)} %get-tuple-element.192, f32[384]{0:T(512)S(1)} %get-tuple-element.189, f32[384]{0:T(512)S(1)} %convolution_reduce_fusion.7), channel_id=1, replica_groups=mesh['filt'=2,'row'=4,'col'=4] {'col'}, use_global_device_ids=true, to_apply=%region_8.9 | all-reduce | flops 1152 | bytes 9216 | tf_op jit(solution)/shard_map/psum | solution.py:64
  75.7 0.6 convolution_reduce_fusion.6
  76.4 8.3 %all-reduce.4 = (f32[384]{0:T(512)S(1)}, f32[384]{0:T(512)S(1)}, f32[384]{0:T(512)S(1)}) all-reduce(f32[384]{0:T(512)S(1)} %get-tuple-element.191, f32[384]{0:T(512)S(1)} %get-tuple-element.190, f32[384]{0:T(512)S(1)} %convolution_reduce_fusion.6), channel_id=1, replica_groups=mesh['filt'=2,'row'=4,'col'=4] {'row'}, use_global_device_ids=true, to_apply=%region_11.12 | all-reduce | flops 1152 | bytes 9216 | tf_op jit(solution)/shard_map/psum | solution.py:65
  84.7 0.5 convolution_reduce_fusion.5
  85.2 10.4 %psum.111 = f32[384]{0:T(512)S(1)} all-reduce(f32[384]{0:T(512)S(1)} %convolution_reduce_fusion.5), channel_id=1, replica_groups=mesh['filt'=2,'row'=4,'col'=4] {'col'}, use_global_device_ids=true, to_apply=%region_12.13 | all-reduce | flops 384 | bytes 3072 | tf_op jit(solution)/shard_map/psum | solution.py:75
  95.6 0.7 convolution_reduce_fusion.4
  96.3 8.8 %psum.112 = f32[384]{0:T(512)S(1)} all-reduce(f32[384]{0:T(512)S(1)} %convolution_reduce_fusion.4), channel_id=1, replica_groups=mesh['filt'=2,'row'=4,'col'=4] {'row'}, use_global_device_ids=true, to_apply=%region_13.14 | all-reduce | flops 384 | bytes 3072 | tf_op jit(solution)/shard_map/psum | solution.py:83
  105.1 0.5 convolution_reduce_fusion.3
  105.6 8.5 %psum.113 = f32[384]{0:T(512)S(1)} all-reduce(f32[384]{0:T(512)S(1)} %convolution_reduce_fusion.3), channel_id=1, replica_groups=mesh['filt'=2,'row'=4,'col'=4] {'col'}, use_global_device_ids=true, to_apply=%region_14.15 | all-reduce | flops 384 | bytes 3072 | tf_op jit(solution)/shard_map/psum | solution.py:75
  114.1 0.7 convolution_reduce_fusion.2
  114.7 8.7 %psum.114 = f32[384]{0:T(512)S(1)} all-reduce(f32[384]{0:T(512)S(1)} %convolution_reduce_fusion.2), channel_id=1, replica_groups=mesh['filt'=2,'row'=4,'col'=4] {'row'}, use_global_device_ids=true, to_apply=%region_15.16 | all-reduce | flops 384 | bytes 3072 | tf_op jit(solution)/shard_map/psum | solution.py:83
  123.4 0.5 convolution_reduce_fusion.1
  123.9 10.4 %psum.115 = f32[384]{0:T(512)S(1)} all-reduce(f32[384]{0:T(512)S(1)} %convolution_reduce_fusion.1), channel_id=1, replica_groups=mesh['filt'=2,'row'=4,'col'=4] {'col'}, use_global_device_ids=true, to_apply=%region_16.17 | all-reduce | flops 384 | bytes 3072 | tf_op jit(solution)/shard_map/psum | solution.py:75
  134.3 0.7 convolution_reduce_fusion
  134.9 8.9 %psum.116 = f32[384]{0:T(512)S(1)} all-reduce(f32[384]{0:T(512)S(1)} %convolution_reduce_fusion), channel_id=1, replica_groups=mesh['filt'=2,'row'=4,'col'=4] {'row'}, use_global_device_ids=true, to_apply=%region_17.18 | all-reduce | flops 384 | bytes 3072 | tf_op jit(solution)/shard_map/psum | solution.py:83
  143.8 0.2 fusion.22
  144.0 0.3 fusion.5
  144.3 0.0 copy-start
  144.3 1.0 fusion.6
  145.3 0.0 all-reduce.7.cloned.1.call-update
  145.3 0.0 reduce-scatter.2.cloned.1.call-start
  145.3 0.9 convolution_convert_fusion
  146.3 0.0 reduce-scatter.2.cloned.1.call-update
  146.3 0.0 copy-done
  146.3 0.7 convert_reduce_fusion
  147.0 37.6 %all-reduce.2 = (f32[]{:T(128)}, f32[]{:T(128)}) all-reduce(f32[]{:T(128)} %get-tuple-element.203, f32[]{:T(128)} %get-tuple-element.202), channel_id=1, replica_groups=mesh['filt'=2,'row'=4,'col'=4] {'row','col'}, use_global_device_ids=true, to_apply=%region_24.25 | all-reduce | flops 2 | bytes 16 | tf_op jit(solution)/shard_map/psum | solution.py:117
  186.6 0.6 subtract_multiply_fusion
  187.2 1.5 add_convert_fusion
  (25 shorter events, 0.1 us)
Async XLA Ops:
  8.0 179.2 %all-reduce.7.cloned.1.call-start = ((), (), s32[]{:S(2)}) async-start(), calls=%async_computation.1 | async-start | bytes 393216 | tf_op jit(solution)/shard_map/psum | solution.py:109
  32.7 9.3 %copy-start.4 = (u32[32]{0:T(128)S(1)}, u32[32]{0:T(128)}, u32[]{:S(2)}) copy-start(u32[32]{0:T(128)} %constant.190) | copy-start | bytes 388
  32.7 10.6 %copy-start.1 = (bf16[96]{0:T(256)(128)(2,1)S(1)}, bf16[96]{0:T(256)(128)(2,1)}, u32[]{:S(2)}) copy-start(bf16[96]{0:T(256)(128)(2,1)} %param.8) | copy-start | bytes 580
  32.7 19.8 %copy-start.3 = (u32[32]{0:T(128)S(1)}, u32[32]{0:T(128)}, u32[]{:S(2)}) copy-start(u32[32]{0:T(128)} %constant.185) | copy-start | bytes 388
  32.7 21.0 %copy-start.2 = (bf16[96]{0:T(256)(128)(2,1)S(1)}, bf16[96]{0:T(256)(128)(2,1)}, u32[]{:S(2)}) copy-start(bf16[96]{0:T(256)(128)(2,1)} %param.7) | copy-start | bytes 580
  144.3 2.0 %copy-start = (bf16[96]{0:T(256)(128)(2,1)S(1)}, bf16[96]{0:T(256)(128)(2,1)}, u32[]{:S(2)}) copy-start(bf16[96]{0:T(256)(128)(2,1)} %param.9) | copy-start | bytes 580
  145.3 41.9 %reduce-scatter.2.cloned.1.call-start = ((), (), s32[]{:S(2)}) async-start(), calls=%async_computation.2 | async-start | bytes 245760 | tf_op jit(solution)/shard_map/reduce_scatter | solution.py:111
Sparse Core Ops, SparseCore 0:
  145.4 31.3 all-reduce.6
Sparse Core Ops, SparseCore 1:
  148.5 20.6 reduce-scatter.1
where the time goes:
time: 197 us; the launch traced here: 196 us
  blocking collectives  164 us (83%)
  between operations  19 us (10%)
  matrix products  7.37 us (4%)
  other arithmetic  3.69 us (2%)
    psum x1, blocking collectives, local(): lax.psum((jnp.sum(own_wts), jnp.sum(own_wts * phi_own)), ('row', 'col'))  37.6 us
    psum x3, blocking collectives, local(): row_total = lax.psum(row_apply.reshape(rows), 'col')  29.3 us
    psum x3, blocking collectives, local(): col_total = lax.psum(col_apply, 'row')  26.4 us
    unnamed x2, blocking collectives  20.9 us
    all_gather x1, blocking collectives, local(): lax.all_gather(particles, 'col', axis=0, tiled=True)  15.7 us
    all_gather x1, blocking collectives, local(): lax.all_gather(particles, 'row', axis=0, tiled=True)  8.96 us
    all_gather x1, blocking collectives, local(): lax.all_gather(cotangent, 'row', axis=0, tiled=True)  8.6 us
    psum x1, blocking collectives, local(): lax.psum((rowmass_part.reshape(rows), rowph_part.reshape(rows)), 'col')  8.49 us
  transfers between devices with their start and end apart: 2, of which 0 were waited for; matrix products, arithmetic and copies ran while one was open for 1% of the time, Pallas kernels for 0%

commit v1 on v0

--- a/solution.py
+++ b/solution.py
@@ -1,6 +1,9 @@
+import functools
 import jax
 import jax.numpy as jnp
 from jax import lax
+from jax.experimental import pallas as pl
+from jax.experimental.pallas import tpu as pltpu
 from jax.sharding import PartitionSpec as P
 
 ITERS = 4
@@ -9,7 +12,7 @@
 EPS = 0.09
 
 
-def local(particles, cotangent, row_potential, col_potential, weights):
+def local_general(particles, cotangent, row_potential, col_potential, weights):
     row_parts, row_fpot, row_wts = (
         lax.all_gather(particles, "col", axis=0, tiled=True),
         lax.all_gather(row_potential, "col", axis=0, tiled=True),
@@ -120,7 +123,307 @@
     return (grad_particles, grad_weights)
 
 
+LANES = 128
+SUBL = 8
+CHUNK = 256
+PLAN_BYTES = 24 * 1024 * 1024
+
+
+def fold(block):
+    return jnp.sum(block.reshape(block.shape[0] // SUBL, SUBL, block.shape[1]), axis=0)
+
+
+def wide(column):
+    return jnp.broadcast_to(column, (column.shape[0], LANES))
+
+
+def fused_kernel(
+    ncol, x_ref, gy_ref, pot_ref, gp_ref, gw_ref,
+    x_all, gy_all, pots, plan, a_col, f_b, w_col, r_col, hr_col, phi_col, a_lane,
+    zs, zr, xs, xr, ps, pr,
+):
+    nrow = 4
+    own = x_ref.shape[0]
+    half = own // 2
+    width = x_ref.shape[1]
+    blocks = nrow * ncol
+    total = own * blocks
+    tiles = total // LANES
+    me_r = lax.axis_index("row")
+    me_c = lax.axis_index("col")
+    me = me_r * ncol + me_c
+    xn = me_r + 1 - 2 * (me_r % 2)
+    yn = (me_r + 2) % nrow
+    dn = (xn + 2) % nrow
+    peers = [(dr, dc) for dr in range(nrow) for dc in range(ncol) if dr or dc]
+
+    def at(row, col, part=None):
+        base = (row * ncol + col) * own
+        if part is None:
+            return pl.ds(pl.multiple_of(base, 32), own)
+        return pl.ds(pl.multiple_of(base + part * half, 16), half)
+
+    def dev(row, col):
+        return {"row": row, "col": col}
+
+    barrier = pltpu.get_barrier_semaphore()
+    for dr, dc in peers:
+        pl.semaphore_signal(
+            barrier, inc=1, device_id=dev((me_r + dr) % nrow, (me_c + dc) % ncol),
+            device_id_type=pl.DeviceIdType.MESH,
+        )
+    x_all[at(me_r, me_c), :] = x_ref[...]
+    gy_all[at(me_r, me_c), :] = gy_ref[...]
+    pots[pl.ds(pl.multiple_of(me * 16, 16), 16), :] = pot_ref[...]
+    pl.semaphore_wait(barrier, len(peers))
+
+    def copy(src, dst, ssem, rsem, row, col):
+        c = pltpu.make_async_remote_copy(
+            src_ref=src, dst_ref=dst, send_sem=ssem, recv_sem=rsem,
+            device_id=dev(row, col), device_id_type=pl.DeviceIdType.MESH,
+        )
+        c.start()
+        return c
+
+    pending = []
+
+    def send_z(buf, ref, n):
+        out = []
+        for dc in range(1, ncol):
+            k = n * (ncol - 1) + dc - 1
+            out.append(copy(ref, buf.at[at(me_r, me_c)], zs.at[k], zr.at[k], me_r, (me_c + dc) % ncol))
+        return out
+
+    def send_xy(buf, n, k):
+        col = (me_c + ncol - k) % ncol
+        s = (n * ncol + k) * 4
+        here = buf.at[at(me_r, col)]
+        return (
+            copy(here, here, xs.at[s], xr.at[s], xn, me_c),
+            copy(here, here, xs.at[s + 1], xr.at[s + 1], yn, me_c),
+        )
+
+    def forward(buf, n, k, first, second):
+        col = (me_c + ncol - k) % ncol
+        s = (n * ncol + k) * 4
+        first.wait_recv()
+        src = buf.at[at(xn, col, 0)]
+        one = copy(src, src, xs.at[s + 2], xr.at[s + 2], yn, me_c)
+        second.wait_recv()
+        src = buf.at[at(yn, col, 1)]
+        two = copy(src, src, xs.at[s + 3], xr.at[s + 3], xn, me_c)
+        return (one, two)
+
+    zx = send_z(x_all, x_ref, 0)
+    xy_x = [send_xy(x_all, 0, 0)]
+    pot_copies = []
+    for k, (dr, dc) in enumerate(peers):
+        pot_copies.append(
+            copy(
+                pot_ref, pots.at[pl.ds(pl.multiple_of(me * 16, 16), 16)], ps.at[k], pr.at[k],
+                (me_r + dr) % nrow, (me_c + dc) % ncol,
+            )
+        )
+    for k in range(1, ncol):
+        zx[k - 1].wait_recv()
+        xy_x.append(send_xy(x_all, 0, k))
+    zg = send_z(gy_all, gy_ref, 1)
+    fw_x = [forward(x_all, 0, k, *xy_x[k]) for k in range(ncol)]
+    xy_g = [send_xy(gy_all, 1, 0)]
+    for c in pot_copies:
+        c.wait_recv()
+
+    scale = 1.0 / (width * EPS)
+    eye = (
+        lax.broadcasted_iota(jnp.int32, (own, LANES), 0)
+        == lax.broadcasted_iota(jnp.int32, (own, LANES), 1)
+    )
+
+    def spread(b, carry):
+        rows = pl.ds(pl.multiple_of(b * own, 32), own)
+        pot = pots[pl.ds(pl.multiple_of(b * 16, 16), 16), :].astype(jnp.float32)
+        for at_row, dst in ((0, a_col), (1, f_b), (2, w_col)):
+            line = jnp.broadcast_to(pot[at_row : at_row + 1, :], (own, LANES))
+            dst[rows, :] = wide(jnp.sum(jnp.where(eye, line, 0.0), axis=1, keepdims=True))
+        return carry
+
+    lax.fori_loop(0, blocks, spread, 0)
+    for k in range(1, ncol):
+        zg[k - 1].wait_recv()
+        xy_g.append(send_xy(gy_all, 1, k))
+    for one, two in fw_x:
+        one.wait_recv()
+        two.wait_recv()
+
+    eye_l = (
+        lax.broadcasted_iota(jnp.int32, (LANES, LANES), 0)
+        == lax.broadcasted_iota(jnp.int32, (LANES, LANES), 1)
+    )
+
+    def to_lanes(column):
+        return jnp.sum(jnp.where(eye_l, column, 0.0), axis=0, keepdims=True)
+
+    b_parts = []
+    for t in range(tiles):
+        rows = pl.ds(t * LANES, LANES)
+        xf = x_all[rows, :].astype(jnp.float32)
+        sq = jnp.sum(xf * xf, axis=1, keepdims=True) * (1.0 / (2.0 * width))
+        a = (a_col[rows, :] - sq) * (1.0 / EPS)
+        b = (f_b[rows, :] - sq) * (1.0 / EPS)
+        a_col[rows, :] = a
+        f_b[rows, :] = b
+        b_parts.append(to_lanes(b))
+        a_lane[0:1, pl.ds(t * LANES, LANES)] = to_lanes(a)
+    b_lane = jnp.concatenate(b_parts, axis=1)
+
+    def nt(left, right):
+        return lax.dot_general(
+            left, right, (((1,), (1,)), ((), ())), preferred_element_type=jnp.float32
+        )
+
+    def cut(value, t):
+        return value[:, t * LANES : (t + 1) * LANES]
+
+    def make_plan(i, acc):
+        rows = pl.ds(pl.multiple_of(i * CHUNK, CHUNK), CHUNK)
+        cross = nt(x_all[rows, :], x_all[...])
+        a = a_col[rows, :]
+        sums = jnp.zeros((CHUNK, LANES), jnp.float32)
+        cols = []
+        for t in range(tiles):
+            p = jnp.exp(cut(cross, t) * scale + (a + cut(b_lane, t)))
+            plan[rows, pl.ds(t * LANES, LANES)] = p
+            sums = sums + p
+            cols.append(fold(p))
+        r_col[rows, :] = wide(jnp.sum(sums, axis=1, keepdims=True))
+        return acc + jnp.concatenate(cols, axis=1)
+
+    zeros = jnp.zeros((SUBL, total), jnp.float32)
+    count = total // CHUNK
+    c_acc = lax.fori_loop(0, count // 2, make_plan, zeros)
+    fw_g = [forward(gy_all, 1, k, *xy_g[k]) for k in range(ncol)]
+    c_acc = lax.fori_loop(count // 2, count, make_plan, c_acc)
+    for one, two in fw_g:
+        one.wait_recv()
+        two.wait_recv()
+    c_lane = jnp.sum(c_acc, axis=0, keepdims=True)
+
+    def first(i, carry):
+        hc, acc = carry
+        rows = pl.ds(pl.multiple_of(i * CHUNK, CHUNK), CHUNK)
+        h = nt(x_all[rows, :], gy_all[...])
+        sums = jnp.zeros((CHUNK, LANES), jnp.float32)
+        cols = []
+        for t in range(tiles):
+            v = plan[rows, pl.ds(t * LANES, LANES)] * cut(h, t)
+            sums = sums + v
+            cols.append(fold(v))
+        hr = wide(jnp.sum(sums, axis=1, keepdims=True))
+        hr_col[rows, :] = hr
+        phi = -hr / r_col[rows, :]
+        more = [fold(plan[rows, pl.ds(t * LANES, LANES)] * phi) for t in range(tiles)]
+        return hc + jnp.concatenate(cols, axis=1), acc + jnp.concatenate(more, axis=1)
+
+    hc_acc, acc = lax.fori_loop(0, count, first, (zeros, zeros))
+    hc_lane = jnp.sum(hc_acc, axis=0, keepdims=True)
+    psi = -(hc_lane + jnp.sum(acc, axis=0, keepdims=True)) / c_lane
+
+    for step in range(1, ITERS):
+
+        def sweep(i, acc):
+            rows = pl.ds(pl.multiple_of(i * CHUNK, CHUNK), CHUNK)
+            sums = jnp.zeros((CHUNK, LANES), jnp.float32)
+            for t in range(tiles):
+                sums = sums + plan[rows, pl.ds(t * LANES, LANES)] * cut(psi, t)
+            phi = -(hr_col[rows, :] + wide(jnp.sum(sums, axis=1, keepdims=True))) / r_col[rows, :]
+            phi_col[rows, :] = phi
+            more = [fold(plan[rows, pl.ds(t * LANES, LANES)] * phi) for t in range(tiles)]
+            return acc + jnp.concatenate(more, axis=1)
+
+        acc = lax.fori_loop(0, count, sweep, zeros)
+        psi = -(hc_lane + jnp.sum(acc, axis=0, keepdims=True)) / c_lane
+
+    mine = at(me_r, me_c)
+    phi_lane = jnp.concatenate([to_lanes(phi_col[pl.ds(t * LANES, LANES), :]) for t in range(tiles)], axis=1)
+    phi_own = phi_col[mine, :]
+    x_own = x_ref[...]
+    gy_own = gy_ref[...]
+    p_own = plan[mine, :]
+    q_own = p_own * (nt(x_own, gy_all[...]) + (phi_own[:, :1] + psi))
+    q_sum = jnp.sum(q_own, axis=1, keepdims=True)
+    rowterm = jnp.dot(p_own.astype(jnp.bfloat16), gy_all[...], preferred_element_type=jnp.float32)
+    mix = jnp.dot(q_own.astype(jnp.bfloat16), x_all[...], preferred_element_type=jnp.float32)
+
+    pick = lax.broadcasted_iota(jnp.int32, (own, total), 1) == (
+        lax.broadcasted_iota(jnp.int32, (own, total), 0) + me * own
+    )
+    psi_own = jnp.sum(jnp.where(pick, psi, 0.0), axis=1, keepdims=True)
+    p_t = jnp.exp(nt(x_own, x_all[...]) * scale + (f_b[mine, :][:, :1] + a_lane[...]))
+    q_t = p_t * (nt(gy_own, x_all[...]) + (psi_own + phi_lane))
+    mix = mix + jnp.dot(q_t.astype(jnp.bfloat16), x_all[...], preferred_element_type=jnp.float32)
+    gp_ref[...] = (rowterm + (mix - q_sum * x_own.astype(jnp.float32)) * scale).astype(jnp.bfloat16)
+
+    w_all = w_col[...]
+    w_sum = jnp.sum(fold(w_all), axis=0, keepdims=True)
+    w_phi = jnp.sum(fold(w_all * phi_col[...]), axis=0, keepdims=True)
+    phi_row = jnp.sum(jnp.where(eye, phi_own, 0.0), axis=0, keepdims=True)
+    gw_ref[...] = (-(total / w_sum) * (phi_row - w_phi / w_sum))[:, :own]
+
+    for c in zx + zg + pot_copies:
+        c.wait_send()
+    for group in (xy_x, fw_x, xy_g, fw_g):
+        for one, two in group:
+            one.wait_send()
+            two.wait_send()
+
+
+def local_fused(ncol, particles, cotangent, row_potential, col_potential, weights):
+    own, width = particles.shape
+    total = own * ncol * 4
+    pot = jnp.pad(
+        jnp.stack([row_potential, col_potential, weights]), ((0, 13), (0, LANES - own))
+    )
+    column = pltpu.VMEM((total, LANES), jnp.float32)
+    dma = pltpu.SemaphoreType.DMA
+    peers = 4 * ncol - 1
+    gp, gw = pl.pallas_call(
+        functools.partial(fused_kernel, ncol),
+        out_shape=(
+            jax.ShapeDtypeStruct((own, width), jnp.bfloat16),
+            jax.ShapeDtypeStruct((1, own), jnp.float32),
+        ),
+        in_specs=[pl.BlockSpec(memory_space=pltpu.VMEM)] * 3,
+        out_specs=[pl.BlockSpec(memory_space=pltpu.VMEM)] * 2,
+        scratch_shapes=[
+            pltpu.VMEM((total, width), jnp.bfloat16),
+            pltpu.VMEM((total, width), jnp.bfloat16),
+            pltpu.VMEM((16 * 4 * ncol, LANES), jnp.bfloat16),
+            pltpu.VMEM((total, total), jnp.float32),
+            column, column, column, column, column, column,
+            pltpu.VMEM((1, total), jnp.float32),
+            dma((2 * (ncol - 1),)), dma((2 * (ncol - 1),)),
+            dma((8 * ncol,)), dma((8 * ncol,)),
+            dma((peers,)), dma((peers,)),
+        ],
+        compiler_params=pltpu.CompilerParams(
+            collective_id=0, has_side_effects=True, vmem_limit_bytes=48 * 1024 * 1024
+        ),
+        cost_estimate=pl.CostEstimate(flops=5 * total * total * width, bytes_accessed=4 * own * width, transcendentals=total * total),
+    )(particles, cotangent, pot)
+    return gp, gw.reshape(own)
+
+
 def solution(mesh):
+    nrow, ncol = mesh.shape["row"], mesh.shape["col"]
+
+    def local(particles, cotangent, row_potential, col_potential, weights):
+        args = (particles, cotangent, row_potential, col_potential, weights)
+        own = particles.shape[0]
+        total = own * nrow * ncol
+        if nrow == 4 and ncol > 1 and own % 32 == 0 and own <= LANES and total % CHUNK == 0 and 4 * total * total <= PLAN_BYTES:
+            return local_fused(ncol, *args)
+        return local_general(*args)
+
     return jax.shard_map(
         local,
         mesh=mesh,

time: 197 us -> 39.8 us (0.20)
  blocking collectives: 164 us -> 0 us
  Pallas kernels: 0 us -> 35.5 us
  between operations: 19 us -> 0.67 us
  matrix products: 7.37 us -> 0 us
  other arithmetic: 3.69 us -> 0.01 us
    psum x9 -> x0, blocking collectives: 110 us -> none  [the longest x1 37.6 us: local(): lax.psum((jnp.sum(own_wts), jnp.sum(own_wts * phi_own)), ('row', 'col'))]
    pallas_call x0 -> x1, Pallas kernels: none -> 35.5 us  [local_fused(): pl.pallas_call(functools.partial(fused_kernel, ncol), out_shape=(jax.Shap...]
    all_gather x3 -> x0, blocking collectives: 33.2 us -> none  [the longest x1 15.7 us: local(): lax.all_gather(particles, 'col', axis=0, tiled=True)]
    unnamed x2 -> x0, blocking collectives: 20.9 us -> none
    dot_general x13 -> x0, matrix products: 7.37 us -> none  [the longest x4 2.61 us: apply_cols(): return (acc + jnp.dot(item[3], plan, precision=lax.Precision.HIGHEST), None)]
  transfers between devices with their start and end apart: 2 -> 0, of which waited for: 0 -> 0; matrix products, arithmetic and copies ran while one was open for 1% -> 0% of each run, Pallas kernels for 0% -> 0%
where the time goes in v1:
time: 39.8 us; the launch traced here: 39.6 us
  Pallas kernels  35.5 us (89%)
  local copies, waits for them, and re-layouts  3.39 us (9%)
  between operations  0.67 us (2%)
    pallas_call x1, Pallas kernels, local_fused(): pl.pallas_call(functools.partial(fused_kernel, ncol), out_shape=(jax.Shap...  35.5 us
    unnamed x12, local copies, waits for them, and re-layouts  3.39 us

profile of v1, /device:TPU:0, one launch (start us, length us, event | category | flops | bytes accessed | tf_op | source)
XLA Modules:
  0.0 39.6 jit_solution(6408080618295339887)
XLA Ops:
  0.6 0.0 copy-start.2
  0.6 0.0 copy-start.3
  0.7 0.0 copy-start.4
  0.7 0.6 %copy-done.2 = bf16[96]{0:T(256)(128)(2,1)S(1)} copy-done((bf16[96]{0:T(256)(128)(2,1)S(1)}, bf16[96]{0:T(256)(128)(2,1)}, u32[]{:S(2)}) %copy-start.2) | copy-done | bytes 216
  1.3 0.0 copy-done.3
  1.3 0.0 copy-done.4
  1.3 0.0 copy-start
  1.3 0.8 %copy-done = bf16[96,256]{1,0:T(8,128)(2,1)S(1)} copy-done((bf16[96,256]{1,0:T(8,128)(2,1)S(1)}, bf16[96,256]{1,0:T(8,128)(2,1)}, u32[]{:S(2)}) %copy-start) | copy-done | bytes 49176
  2.1 0.0 copy-start.1
  2.1 0.8 %copy-done.1 = bf16[96,256]{1,0:T(8,128)(2,1)S(1)} copy-done((bf16[96,256]{1,0:T(8,128)(2,1)S(1)}, bf16[96,256]{1,0:T(8,128)(2,1)}, u32[]{:S(2)}) %copy-start.1) | copy-done | bytes 49176
  2.9 35.5 %shard_map.68 = (bf16[96,256]{1,0:T(8,128)(2,1)S(1)}, f32[1,96]{1,0:T(1,128)S(1)}) custom-call(bf16[96,256]{1,0:T(8,128)(2,1)S(1)} %copy-done, bf16[96,256]{1,0:T(8,128)(2,1)S(1)} %copy-done.1, bf16[16,128]{1,0:T(8,128)(2,1)S(1)} %fusion.8.pot_ref), custom_call_target="tpu_custom_call" | custom-call | flops 3019898880 | bytes 98304 | tf_op jit(solution)/shard_map/pallas_call | solution.py:389
  38.4 0.6 %copy.9 = bf16[96,256]{1,0:T(8,128)(2,1)} copy(bf16[96,256]{1,0:T(8,128)(2,1)S(1)} %get-tuple-element.8) | data formatting | bytes 98304
  39.1 0.5 %copy.10 = f32[96]{0:T(128)} copy(f32[96]{0:T(128)S(1)} %bitcast.4) | data formatting | bytes 768
  (1 shorter events, 0.0 us)
Async XLA Ops:
  0.6 0.7 %copy-start.2 = (bf16[96]{0:T(256)(128)(2,1)S(1)}, bf16[96]{0:T(256)(128)(2,1)}, u32[]{:S(2)}) copy-start(bf16[96]{0:T(256)(128)(2,1)} %param.9) | copy-start | bytes 580
  0.6 0.7 %copy-start.3 = (bf16[96]{0:T(256)(128)(2,1)S(1)}, bf16[96]{0:T(256)(128)(2,1)}, u32[]{:S(2)}) copy-start(bf16[96]{0:T(256)(128)(2,1)} %param.8) | copy-start | bytes 580
  0.7 0.7 %copy-start.4 = (bf16[96]{0:T(256)(128)(2,1)S(1)}, bf16[96]{0:T(256)(128)(2,1)}, u32[]{:S(2)}) copy-start(bf16[96]{0:T(256)(128)(2,1)} %param.7) | copy-start | bytes 580
  1.3 0.8 %copy-start = (bf16[96,256]{1,0:T(8,128)(2,1)S(1)}, bf16[96,256]{1,0:T(8,128)(2,1)}, u32[]{:S(2)}) copy-start(bf16[96,256]{1,0:T(8,128)(2,1)} %x_ref.1) | copy-start | bytes 147460
  2.1 0.8 %copy-start.1 = (bf16[96,256]{1,0:T(8,128)(2,1)S(1)}, bf16[96,256]{1,0:T(8,128)(2,1)}, u32[]{:S(2)}) copy-start(bf16[96,256]{1,0:T(8,128)(2,1)} %gy_ref.1) | copy-start | bytes 147460

commit v2 on v1

v2 whole, which is shorter than its diff:
```python
import functools
import jax
import jax.numpy as jnp
from jax import lax
from jax.experimental import pallas as pl
from jax.experimental.pallas import tpu as pltpu
from jax.sharding import PartitionSpec as P

ITERS = 4


EPS = 0.09


def local_general(particles, cotangent, row_potential, col_potential, weights):
    row_parts, row_fpot, row_wts = (
        lax.all_gather(particles, "col", axis=0, tiled=True),
        lax.all_gather(row_potential, "col", axis=0, tiled=True),
        lax.all_gather(weights, "col", axis=0, tiled=True),
    )
    col_parts, col_grads, col_gpot = (
        lax.all_gather(particles, "row", axis=0, tiled=True),
        lax.all_gather(cotangent, "row", axis=0, tiled=True),
        lax.all_gather(col_potential, "row", axis=0, tiled=True),
    )
    own = particles.shape[0]
    width = particles.shape[1]
    rows = row_parts.shape[0]
    cols = col_parts.shape[0]
    blk = 512 if rows % 512 == 0 else rows
    count = rows // blk
    row_float = row_parts.astype(jnp.float32)
    row_sq = jnp.sum(row_float * row_float, axis=1)
    col_float = col_parts.astype(jnp.float32)
    col_sq = jnp.sum(col_float * col_float, axis=1)
    fpot = row_fpot.astype(jnp.float32)
    gpot = col_gpot.astype(jnp.float32)
    stacked = jnp.concatenate([col_parts, col_grads], axis=0)
    items = (
        row_parts.reshape(count, blk, width),
        fpot.reshape(count, blk),
        row_sq.reshape(count, blk),
    )

    def plan_from(cross, pot_blk, sq_blk):
        cost = (sq_blk[:, None] + col_sq[None, :] - 2.0 * cross) / (2.0 * width)
        return jnp.exp((pot_blk[:, None] + gpot[None, :] - cost) / EPS)

    def plan_only(part_blk, pot_blk, sq_blk):
        cross = jnp.einsum("rd,cd->rc", part_blk, col_parts, preferred_element_type=jnp.float32)
        return plan_from(cross, pot_blk, sq_blk)

    def first(carry, item):
        part_blk, pot_blk, sq_blk = item
        both = jnp.einsum("rd,cd->rc", part_blk, stacked, preferred_element_type=jnp.float32)
        plan = plan_from(both[:, :cols], pot_blk, sq_blk)
        weighted = plan * both[:, cols:]
        return (
            (carry[0] + jnp.sum(plan, axis=0), carry[1] + jnp.sum(weighted, axis=0)),
            (jnp.sum(plan, axis=1), jnp.sum(weighted, axis=1)),
        )

    zeros_c = jnp.zeros((cols,), jnp.float32)
    (colmass_part, colph_part), (rowmass_part, rowph_part) = lax.scan(
        first, (zeros_c, zeros_c), items
    )
    rowmass, rowph = lax.psum((rowmass_part.reshape(rows), rowph_part.reshape(rows)), "col")
    colmass, colph = lax.psum((colmass_part, colph_part), "row")
    psi = zeros_c
    phi = jnp.zeros((rows,), jnp.float32)
    for step in range(ITERS):

        def apply_rows(carry, item):
            plan = plan_only(item[0], item[1], item[2])
            return (carry, jnp.dot(plan, psi, precision=lax.Precision.HIGHEST))

        unused, row_apply = lax.scan(apply_rows, jnp.zeros((), jnp.float32), items)
        row_total = lax.psum(row_apply.reshape(rows), "col")
        phi = -(rowph + row_total) / rowmass

        def apply_cols(acc, item):
            plan = plan_only(item[0], item[1], item[2])
            return (acc + jnp.dot(item[3], plan, precision=lax.Precision.HIGHEST), None)

        col_apply, unused_out = lax.scan(apply_cols, zeros_c, items + (phi.reshape(count, blk),))
        col_total = lax.psum(col_apply, "row")
        psi = -(colph + col_total) / colmass

    def last(acc, item):
        part_blk, pot_blk, sq_blk, phi_blk = item
        both = jnp.einsum("rd,cd->rc", part_blk, stacked, preferred_element_type=jnp.float32)
        plan = plan_from(both[:, :cols], pot_blk, sq_blk)
        mixed = plan * (both[:, cols:] + phi_blk[:, None] + psi[None, :])
        qrow = jnp.sum(mixed, axis=1)
        plan_bf = plan.astype(jnp.bfloat16)
        mixed_bf = mixed.astype(jnp.bfloat16)
        rowterm = jnp.dot(plan_bf, col_grads, preferred_element_type=jnp.float32)
        rowterm = rowterm + (
            jnp.dot(mixed_bf, col_parts, preferred_element_type=jnp.float32)
            - qrow[:, None] * part_blk.astype(jnp.float32)
        ) / (width * EPS)
        return (
            acc + jnp.einsum("rc,rd->cd", mixed_bf, part_blk, preferred_element_type=jnp.float32),
            rowterm,
        )

    col_acc, row_terms = lax.scan(
        last, jnp.zeros((cols, width), jnp.float32), items + (phi.reshape(count, blk),)
    )
    row_terms = row_terms.reshape(rows, width)
    start = lax.axis_index("col") * own
    summed = lax.psum(row_terms.astype(jnp.bfloat16), "col").astype(jnp.float32)
    row_own = lax.dynamic_slice_in_dim(summed, start, own, 0)
    col_own = lax.psum_scatter(
        col_acc.astype(jnp.bfloat16), "row", scatter_dimension=0, tiled=True
    ).astype(jnp.float32)
    grad_particles = (row_own + col_own / (width * EPS)).astype(jnp.bfloat16)
    phi_own = lax.dynamic_slice_in_dim(phi, start, own, 0)
    own_wts = weights.astype(jnp.float32)
    total, wphi = lax.psum((jnp.sum(own_wts), jnp.sum(own_wts * phi_own)), ("row", "col"))
    count_all = rows * lax.axis_size("row")
    grad_weights = -(count_all / total) * (phi_own - wphi / total)
    return (grad_particles, grad_weights)


LANES = 128
SUBL = 8
SUB = 64
PLAN_BYTES = 24 * 1024 * 1024


def fold(block):
    return jnp.sum(block.reshape(block.shape[0] // SUBL, SUBL, block.shape[1]), axis=0)


def wide(column):
    return jnp.broadcast_to(column, (column.shape[0], LANES))


def nt(left, right):
    return lax.dot_general(
        left, right, (((1,), (1,)), ((), ())), preferred_element_type=jnp.float32
    )


def fused_kernel(
    ncol, x_ref, gy_ref, pot_ref, gp_ref, gw_ref,
    x_all, gy_all, pots, plan, a_col, b_col, w_col, c_col, nhc_col, psi_col,
    a_lane, b_lane, w_lane, r_acc, sums_all,
    ls, zs, zr, xs, xr, ps, pr, hs, hr_sem,
):
    nrow = 4
    own = x_ref.shape[0]
    half = own // 2
    width = x_ref.shape[1]
    blocks = nrow * ncol
    total = own * blocks
    group = own * ncol
    tiles = total // LANES
    me_r = lax.axis_index("row")
    me_c = lax.axis_index("col")
    me = me_r * ncol + me_c
    xn = me_r + 1 - 2 * (me_r % 2)
    yn = (me_r + 2) % nrow
    dn = (xn + 2) % nrow
    peers = [(dr, dc) for dr in range(nrow) for dc in range(ncol) if dr or dc]
    scale = 1.0 / (width * EPS)

    def at(row, col, part=None):
        base = (row * ncol + col) * own
        if part is None:
            return pl.ds(pl.multiple_of(base, 32), own)
        return pl.ds(pl.multiple_of(base + part * half, 16), half)

    def dev(row, col):
        return {"row": row, "col": col}

    mine = at(me_r, me_c)
    local_x = pltpu.make_async_copy(x_ref, x_all.at[mine], ls.at[0])
    local_x.start()
    local_g = pltpu.make_async_copy(gy_ref, gy_all.at[mine], ls.at[1])
    local_g.start()
    barrier = pltpu.get_barrier_semaphore()
    for dr, dc in peers:
        pl.semaphore_signal(
            barrier, inc=1, device_id=dev((me_r + dr) % nrow, (me_c + dc) % ncol),
            device_id_type=pl.DeviceIdType.MESH,
        )
    my_pot = pl.ds(pl.multiple_of(me * 16, 16), 16)
    pots[my_pot, :] = pot_ref[...]
    r_acc[...] = jnp.zeros_like(r_acc)
    c_col[...] = jnp.zeros_like(c_col)
    pl.semaphore_wait(barrier, len(peers))

    def copy(src, dst, ssem, rsem, row, col):
        c = pltpu.make_async_remote_copy(
            src_ref=src, dst_ref=dst, send_sem=ssem, recv_sem=rsem,
            device_id=dev(row, col), device_id_type=pl.DeviceIdType.MESH,
        )
        c.start()
        return c

    def send_z(buf, ref, n):
        out = []
        for dc in range(1, ncol):
            k = n * (ncol - 1) + dc - 1
            out.append(copy(ref, buf.at[mine], zs.at[k], zr.at[k], me_r, (me_c + dc) % ncol))
        return out

    def send_xy(buf, ref, n, k):
        here = buf.at[at(me_r, (me_c + ncol - k) % ncol)]
        src = ref if k == 0 else here
        s = (n * ncol + k) * 4
        return (
            copy(src, here, xs.at[s], xr.at[s], xn, me_c),
            copy(src, here, xs.at[s + 1], xr.at[s + 1], yn, me_c),
        )

    def forward(buf, n, k, first, second):
        col = (me_c + ncol - k) % ncol
        s = (n * ncol + k) * 4
        first.wait_recv()
        src = buf.at[at(xn, col, 0)]
        one = copy(src, src, xs.at[s + 2], xr.at[s + 2], yn, me_c)
        second.wait_recv()
        src = buf.at[at(yn, col, 1)]
        two = copy(src, src, xs.at[s + 3], xr.at[s + 3], xn, me_c)
        return (one, two)

    zx = send_z(x_all, x_ref, 0)
    xy_x = [send_xy(x_all, x_ref, 0, 0)]
    pot_copies = []
    for k, (dr, dc) in enumerate(peers):
        pot_copies.append(
            copy(pot_ref, pots.at[my_pot], ps.at[k], pr.at[k], (me_r + dr) % nrow, (me_c + dc) % ncol)
        )
    for k in range(1, ncol):
        zx[k - 1].wait_recv()
        xy_x.append(send_xy(x_all, x_ref, 0, k))
    zg = send_z(gy_all, gy_ref, 1)
    for c in pot_copies:
        c.wait_recv()

    eye = (
        lax.broadcasted_iota(jnp.int32, (own, LANES), 0)
        == lax.broadcasted_iota(jnp.int32, (own, LANES), 1)
    )
    eye_l = (
        lax.broadcasted_iota(jnp.int32, (LANES, LANES), 0)
        == lax.broadcasted_iota(jnp.int32, (LANES, LANES), 1)
    )

    def to_lanes(column):
        return jnp.sum(jnp.where(eye_l, column, 0.0), axis=0, keepdims=True)

    def to_column(line):
        return jnp.sum(jnp.where(eye, jnp.broadcast_to(line, (own, LANES)), 0.0), axis=1, keepdims=True)

    def spread(b, carry):
        rows = pl.ds(pl.multiple_of(b * own, 32), own)
        pot = pots[pl.ds(pl.multiple_of(b * 16, 16), 16), :].astype(jnp.float32)
        for k, dst in ((0, a_col), (1, b_col), (2, w_col)):
            dst[rows, :] = wide(to_column(pot[k : k + 1, :]))
        return carry

    lax.fori_loop(0, blocks, spread, 0)
    local_x.wait()

    def prepare(g):
        for t in range(group // LANES):
            rows = pl.ds(pl.multiple_of(g * group + t * LANES, LANES), LANES)
            xf = x_all[rows, :].astype(jnp.float32)
            sq = jnp.sum(xf * xf, axis=1, keepdims=True) * (1.0 / (2.0 * width))
            a = (a_col[rows, :] - sq) * (1.0 / EPS)
            b = (b_col[rows, :] - sq) * (1.0 / EPS)
            a_col[rows, :] = a
            b_col[rows, :] = b
            a_lane[0:1, rows] = to_lanes(a)
            b_lane[0:1, rows] = to_lanes(b)
            w_lane[0:1, rows] = to_lanes(w_col[rows, :])

    def build(gj, gi):
        down = pl.ds(pl.multiple_of(gj * group, LANES), group)
        over = pl.ds(pl.multiple_of(gi * group, LANES), group)
        cross = nt(x_all[down, :], x_all[over, :])
        accs = [jnp.zeros((SUBL, LANES), jnp.float32)] * (group // LANES)
        for s in range(group // SUB):
            rows = pl.ds(pl.multiple_of(gj * group + s * SUB, SUB), SUB)
            b = b_col[rows, :]
            part = jnp.zeros((SUB, LANES), jnp.float32)
            for t in range(group // LANES):
                lanes = pl.ds(pl.multiple_of(gi * group + t * LANES, LANES), LANES)
                piece = cross[s * SUB : (s + 1) * SUB, t * LANES : (t + 1) * LANES]
                p = jnp.exp(piece * scale + (b + a_lane[0:1, lanes]))
                plan[rows, lanes] = p
                part = part + p
                accs[t] = accs[t] + fold(p)
            c_col[rows, :] += wide(jnp.sum(part, axis=1, keepdims=True))
        for t in range(group // LANES):
            lanes = pl.ds(pl.multiple_of(gi * group + t * LANES, LANES), LANES)
            r_acc[:, lanes] += accs[t]

    def near(u):
        return (me_r // 2 + u // 2) % 2 * 2 + (me_r % 2 + u % 2) % 2

    prepare(me_r)
    build(me_r, me_r)
    fw_x = [forward(x_all, 0, k, *xy_x[k]) for k in range(ncol)]
    prepare(xn)
    prepare(yn)

    def early(i, carry):
        build(near(i // 3), near(i % 3))
        return carry

    lax.fori_loop(1, 9, early, 0)
    for one, two in fw_x:
        one.wait_recv()
        two.wait_recv()
    prepare(dn)

    x_own = x_all[mine, :]
    local_g.wait()
    cross_own = nt(x_own, x_all[...]) * scale
    pt_own = jnp.exp(cross_own + (b_col[mine, :][:, :1] + a_lane[...]))
    ht_own = nt(gy_all[mine, :], x_all[...])
    ph = pt_own * ht_own
    hc_own = jnp.sum(ph, axis=1, keepdims=True)
    slot = sums_all.at[me]
    slot[:, pl.ds(0, total)] = jnp.sum(fold(ph), axis=0, keepdims=True)
    slot[:, pl.ds(total, LANES)] = jnp.sum(jnp.where(eye, hc_own, 0.0), axis=0, keepdims=True)
    sum_copies = []
    for k, (dr, dc) in enumerate(peers):
        sum_copies.append(
            copy(slot, slot, hs.at[k], hr_sem.at[k], (me_r + dr) % nrow, (me_c + dc) % ncol)
        )
    xy_g = [send_xy(gy_all, gy_ref, 1, 0)]
    for k in range(1, ncol):
        zg[k - 1].wait_recv()
        xy_g.append(send_xy(gy_all, gy_ref, 1, k))

    def late(i, carry):
        build(near(jnp.minimum(i, 3)), near(jnp.minimum(6 - i, 3)))
        return carry

    lax.fori_loop(0, 7, late, 0)
    for c in sum_copies:
        c.wait_recv()

    def masses(b, carry):
        rows = pl.ds(pl.multiple_of(b * own, 32), own)
        inv = 1.0 / c_col[rows, :]
        c_col[rows, :] = inv
        nhc_col[rows, :] = -wide(to_column(sums_all[b, :, pl.ds(total, LANES)])) * inv
        return carry

    lax.fori_loop(0, blocks, masses, 0)
    hr = jnp.sum(sums_all[:, :, pl.ds(0, total)], axis=0)
    inv_r = 1.0 / jnp.sum(r_acc[...], axis=0, keepdims=True)
    phi = -hr * inv_r
    zeros = jnp.zeros((SUBL, total), jnp.float32)

    def cut(value, t):
        return value[:, t * LANES : (t + 1) * LANES]

    def psi_of(i, phi):
        for s in range(group // SUB):
            rows = pl.ds(pl.multiple_of(i * group + s * SUB, SUB), SUB)
            part = plan[rows, pl.ds(0, LANES)] * cut(phi, 0)
            for t in range(1, tiles):
                part = part + plan[rows, pl.ds(t * LANES, LANES)] * cut(phi, t)
            total_s = wide(jnp.sum(part, axis=1, keepdims=True))
            psi_col[rows, :] = nhc_col[rows, :] - total_s * c_col[rows, :]

    def sweep(phi):
        def body(i, acc):
            psi_of(i, phi)
            accs = [cut(acc, t) for t in range(tiles)]
            for s in range(group // SUB):
                rows = pl.ds(pl.multiple_of(i * group + s * SUB, SUB), SUB)
                psi = psi_col[rows, :]
                for t in range(tiles):
                    accs[t] = accs[t] + fold(plan[rows, pl.ds(t * LANES, LANES)] * psi)
            return jnp.concatenate(accs, axis=1)

        acc = lax.fori_loop(0, nrow, body, zeros)
        return -(hr + jnp.sum(acc, axis=0, keepdims=True)) * inv_r

    fw_g = []
    for step in range(1, ITERS):
        phi = sweep(phi)
        if step == ITERS - 2:
            fw_g = [forward(gy_all, 1, k, *xy_g[k]) for k in range(ncol)]

    def last(i, carry):
        psi_of(i, phi)
        return carry

    lax.fori_loop(0, nrow, last, 0)
    psi_lane = jnp.concatenate(
        [to_lanes(psi_col[pl.ds(t * LANES, LANES), :]) for t in range(tiles)], axis=1
    )
    pick = lax.broadcasted_iota(jnp.int32, (own, total), 1) == (
        lax.broadcasted_iota(jnp.int32, (own, total), 0) + me * own
    )
    phi_own = jnp.sum(jnp.where(pick, phi, 0.0), axis=1, keepdims=True)
    psi_own = psi_col[mine, :][:, :1]
    q_t = pt_own * (ht_own + (psi_own + phi))
    mix = jnp.dot(q_t.astype(jnp.bfloat16), x_all[...], preferred_element_type=jnp.float32)
    p_own = jnp.exp(cross_own + (a_col[mine, :][:, :1] + b_lane[...]))

    w_all = w_lane[...]
    w_sum = jnp.sum(w_all, axis=1, keepdims=True)
    w_phi = jnp.sum(w_all * phi, axis=1, keepdims=True)
    phi_row = jnp.sum(jnp.where(eye, phi_own, 0.0), axis=0, keepdims=True)
    gw_ref[...] = (-(total / w_sum) * (phi_row - w_phi / w_sum))[:, :own]

    for one, two in fw_g:
        one.wait_recv()
        two.wait_recv()
    q_own = p_own * (nt(x_own, gy_all[...]) + (phi_own + psi_lane))
    q_sum = jnp.sum(q_own, axis=1, keepdims=True)
    rowterm = jnp.dot(p_own.astype(jnp.bfloat16), gy_all[...], preferred_element_type=jnp.float32)
    mix = mix + jnp.dot(q_own.astype(jnp.bfloat16), x_all[...], preferred_element_type=jnp.float32)
    gp_ref[...] = (rowterm + (mix - q_sum * x_own.astype(jnp.float32)) * scale).astype(jnp.bfloat16)

    for c in zx + zg + pot_copies + sum_copies:
        c.wait_send()
    for pairs in (xy_x, fw_x, xy_g, fw_g):
        for one, two in pairs:
            one.wait_send()
            two.wait_send()


def local_fused(ncol, particles, cotangent, row_potential, col_potential, weights):
    own, width = particles.shape
    blocks = 4 * ncol
    total = own * blocks
    pot = jnp.pad(
        jnp.stack([row_potential, col_potential, weights]), ((0, 13), (0, LANES - own))
    )
    column = pltpu.VMEM((total, LANES), jnp.float32)
    line = pltpu.VMEM((1, total), jnp.float32)
    dma = pltpu.SemaphoreType.DMA
    vmem = pl.BlockSpec(memory_space=pltpu.VMEM)
    hbm = pl.BlockSpec(memory_space=pltpu.HBM)
    gp, gw = pl.pallas_call(
        functools.partial(fused_kernel, ncol),
        out_shape=(
            jax.ShapeDtypeStruct((own, width), jnp.bfloat16),
            jax.ShapeDtypeStruct((1, own), jnp.float32),
        ),
        in_specs=[hbm, hbm, vmem],
        out_specs=[vmem, vmem],
        scratch_shapes=[
            pltpu.VMEM((total, width), jnp.bfloat16),
            pltpu.VMEM((total, width), jnp.bfloat16),
            pltpu.VMEM((16 * blocks, LANES), jnp.bfloat16),
            pltpu.VMEM((total, total), jnp.float32),
            column, column, column, column, column, column,
            line, line, line,
            pltpu.VMEM((SUBL, total), jnp.float32),
            pltpu.VMEM((blocks, 1, total + LANES), jnp.float32),
            dma((2,)),
            dma((2 * (ncol - 1),)), dma((2 * (ncol - 1),)),
            dma((8 * ncol,)), dma((8 * ncol,)),
            dma((blocks - 1,)), dma((blocks - 1,)),
            dma((blocks - 1,)), dma((blocks - 1,)),
        ],
        compiler_params=pltpu.CompilerParams(
            collective_id=0, has_side_effects=True, vmem_limit_bytes=48 * 1024 * 1024
        ),
        cost_estimate=pl.CostEstimate(
            flops=3 * total * total * width, bytes_accessed=4 * own * width, transcendentals=total * total
        ),
    )(particles, cotangent, pot)
    return gp, gw.reshape(own)


def solution(mesh):
    nrow, ncol = mesh.shape["row"], mesh.shape["col"]

    def local(particles, cotangent, row_potential, col_potential, weights):
        args = (particles, cotangent, row_potential, col_potential, weights)
        own = particles.shape[0]
        total = own * nrow * ncol
        fits = own % 32 == 0 and own <= LANES and own * ncol % LANES == 0
        if nrow == 4 and ncol > 1 and fits and 4 * total * total <= PLAN_BYTES:
            return local_fused(ncol, *args)
        return local_general(*args)

    return jax.shard_map(
        local,
        mesh=mesh,
        in_specs=(
            P(("filt", "row", "col"), None),
            P(("filt", "row", "col"), None),
            P(("filt", "row", "col")),
            P(("filt", "row", "col")),
            P(("filt", "row", "col")),
        ),
        out_specs=(P(("filt", "row", "col"), None), P(("filt", "row", "col"))),
        check_vma=False,
    )
```

time: 39.8 us -> 42.1 us (1.058)
  Pallas kernels: 35.5 us -> 37.8 us
    pallas_call x1, Pallas kernels: 35.5 us -> 37.8 us  [local_fused(): pl.pallas_call(functools.partial(fused_kernel, ncol), out_shape=(jax.Shap...]
where the time goes in v2:
time: 42.1 us; the launch traced here: 41.9 us
  Pallas kernels  37.8 us (90%)
  local copies, waits for them, and re-layouts  3.39 us (8%)
  between operations  0.67 us (2%)
    pallas_call x1, Pallas kernels, local_fused(): pl.pallas_call(functools.partial(fused_kernel, ncol), out_shape=(jax.Shap...  37.8 us
    unnamed x12, local copies, waits for them, and re-layouts  3.39 us

profile of v2, /device:TPU:0, one launch (start us, length us, event | category | flops | bytes accessed | tf_op | source)
XLA Modules:
  0.0 41.9 jit_solution(4405466234389250343)
XLA Ops:
  0.6 0.0 copy-start.2
  0.6 0.0 copy-start.3
  0.7 0.0 copy-start.4
  0.7 0.6 %copy-done.2 = bf16[96]{0:T(256)(128)(2,1)S(1)} copy-done((bf16[96]{0:T(256)(128)(2,1)S(1)}, bf16[96]{0:T(256)(128)(2,1)}, u32[]{:S(2)}) %copy-start.2) | copy-done | bytes 216
  1.3 0.0 copy-done.3
  1.3 0.0 copy-done.4
  1.3 0.0 copy-start
  1.3 0.8 %copy-done = bf16[96,256]{1,0:T(8,128)(2,1)S(1)} copy-done((bf16[96,256]{1,0:T(8,128)(2,1)S(1)}, bf16[96,256]{1,0:T(8,128)(2,1)}, u32[]{:S(2)}) %copy-start) | copy-done | bytes 49176
  2.1 0.0 copy-start.1
  2.1 0.8 %copy-done.1 = bf16[96,256]{1,0:T(8,128)(2,1)S(1)} copy-done((bf16[96,256]{1,0:T(8,128)(2,1)S(1)}, bf16[96,256]{1,0:T(8,128)(2,1)}, u32[]{:S(2)}) %copy-start.1) | copy-done | bytes 49176
  2.9 37.8 %shard_map.68 = (bf16[96,256]{1,0:T(8,128)(2,1)S(1)}, f32[1,96]{1,0:T(1,128)S(1)}) custom-call(bf16[96,256]{1,0:T(8,128)(2,1)S(1)} %copy-done, bf16[96,256]{1,0:T(8,128)(2,1)S(1)} %copy-done.1, bf16[16,128]{1,0:T(8,128)(2,1)S(1)} %fusion.8.pot_ref), custom_call_target="tpu_custom_call" | custom-call | flops 1811939328 | bytes 98304 | tf_op jit(solution)/shard_map/pallas_call | solution.py:447
  40.8 0.6 %copy.9 = bf16[96,256]{1,0:T(8,128)(2,1)} copy(bf16[96,256]{1,0:T(8,128)(2,1)S(1)} %get-tuple-element.8) | data formatting | bytes 98304
  41.4 0.5 %copy.10 = f32[96]{0:T(128)} copy(f32[96]{0:T(128)S(1)} %bitcast.4) | data formatting | bytes 768
  (1 shorter events, 0.0 us)
Async XLA Ops:
  0.6 0.7 %copy-start.2 = (bf16[96]{0:T(256)(128)(2,1)S(1)}, bf16[96]{0:T(256)(128)(2,1)}, u32[]{:S(2)}) copy-start(bf16[96]{0:T(256)(128)(2,1)} %param.9) | copy-start | bytes 580
  0.6 0.7 %copy-start.3 = (bf16[96]{0:T(256)(128)(2,1)S(1)}, bf16[96]{0:T(256)(128)(2,1)}, u32[]{:S(2)}) copy-start(bf16[96]{0:T(256)(128)(2,1)} %param.8) | copy-start | bytes 580
  0.7 0.7 %copy-start.4 = (bf16[96]{0:T(256)(128)(2,1)S(1)}, bf16[96]{0:T(256)(128)(2,1)}, u32[]{:S(2)}) copy-start(bf16[96]{0:T(256)(128)(2,1)} %param.7) | copy-start | bytes 580
  1.3 0.8 %copy-start = (bf16[96,256]{1,0:T(8,128)(2,1)S(1)}, bf16[96,256]{1,0:T(8,128)(2,1)}, u32[]{:S(2)}) copy-start(bf16[96,256]{1,0:T(8,128)(2,1)} %x_ref.1) | copy-start | bytes 147460
  2.1 0.8 %copy-start.1 = (bf16[96,256]{1,0:T(8,128)(2,1)S(1)}, bf16[96,256]{1,0:T(8,128)(2,1)}, u32[]{:S(2)}) copy-start(bf16[96,256]{1,0:T(8,128)(2,1)} %gy_ref.1) | copy-start | bytes 147460

commit v3 on v2

--- a/solution.py
+++ b/solution.py
@@ -146,7 +146,7 @@
 def fused_kernel(
     ncol, x_ref, gy_ref, pot_ref, gp_ref, gw_ref,
     x_all, gy_all, pots, plan, a_col, b_col, w_col, c_col, nhc_col, psi_col,
-    a_lane, b_lane, w_lane, r_acc, sums_all,
+    a_lane, b_lane, w_lane, r_acc, sums_z, sums_xy,
     ls, zs, zr, xs, xr, ps, pr, hs, hr_sem,
 ):
     nrow = 4
@@ -163,7 +163,7 @@
     xn = me_r + 1 - 2 * (me_r % 2)
     yn = (me_r + 2) % nrow
     dn = (xn + 2) % nrow
-    peers = [(dr, dc) for dr in range(nrow) for dc in range(ncol) if dr or dc]
+    peers = [(me_r, (me_c + dc) % ncol) for dc in range(1, ncol)] + [(xn, me_c), (yn, me_c), (dn, me_c)]
     scale = 1.0 / (width * EPS)
 
     def at(row, col, part=None):
@@ -181,10 +181,9 @@
     local_g = pltpu.make_async_copy(gy_ref, gy_all.at[mine], ls.at[1])
     local_g.start()
     barrier = pltpu.get_barrier_semaphore()
-    for dr, dc in peers:
+    for row, col in peers:
         pl.semaphore_signal(
-            barrier, inc=1, device_id=dev((me_r + dr) % nrow, (me_c + dc) % ncol),
-            device_id_type=pl.DeviceIdType.MESH,
+            barrier, inc=1, device_id=dev(row, col), device_id_type=pl.DeviceIdType.MESH
         )
     my_pot = pl.ds(pl.multiple_of(me * 16, 16), 16)
     pots[my_pot, :] = pot_ref[...]
@@ -192,11 +191,14 @@
     c_col[...] = jnp.zeros_like(c_col)
     pl.semaphore_wait(barrier, len(peers))
 
-    def copy(src, dst, ssem, rsem, row, col):
-        c = pltpu.make_async_remote_copy(
+    def plan_copy(src, dst, ssem, rsem, row, col):
+        return pltpu.make_async_remote_copy(
             src_ref=src, dst_ref=dst, send_sem=ssem, recv_sem=rsem,
             device_id=dev(row, col), device_id_type=pl.DeviceIdType.MESH,
         )
+
+    def copy(*args):
+        c = plan_copy(*args)
         c.start()
         return c
 
@@ -216,29 +218,36 @@
             copy(src, here, xs.at[s + 1], xr.at[s + 1], yn, me_c),
         )
 
-    def forward(buf, n, k, first, second):
+    def forward(buf, n, k):
         col = (me_c + ncol - k) % ncol
         s = (n * ncol + k) * 4
-        first.wait_recv()
         src = buf.at[at(xn, col, 0)]
-        one = copy(src, src, xs.at[s + 2], xr.at[s + 2], yn, me_c)
-        second.wait_recv()
+        one = plan_copy(src, src, xs.at[s + 2], xr.at[s + 2], yn, me_c)
         src = buf.at[at(yn, col, 1)]
-        two = copy(src, src, xs.at[s + 3], xr.at[s + 3], xn, me_c)
+        two = plan_copy(src, src, xs.at[s + 3], xr.at[s + 3], xn, me_c)
         return (one, two)
+
+    def start_forward(pair, group_pair):
+        for came, goes in zip(pair, group_pair):
+            came.wait_recv()
+            goes.start()
 
     zx = send_z(x_all, x_ref, 0)
     xy_x = [send_xy(x_all, x_ref, 0, 0)]
-    pot_copies = []
-    for k, (dr, dc) in enumerate(peers):
-        pot_copies.append(
-            copy(pot_ref, pots.at[my_pot], ps.at[k], pr.at[k], (me_r + dr) % nrow, (me_c + dc) % ncol)
-        )
+    pot_z = [
+        copy(pot_ref, pots.at[my_pot], ps.at[k], pr.at[k], *peers[k]) for k in range(ncol - 1)
+    ]
     for k in range(1, ncol):
         zx[k - 1].wait_recv()
         xy_x.append(send_xy(x_all, x_ref, 0, k))
+    for c in pot_z:
+        c.wait_recv()
+    column_pots = pots.at[pl.ds(pl.multiple_of(me_r * 16 * ncol, 16), 16 * ncol)]
+    pot_xy = [
+        copy(column_pots, column_pots, ps.at[k], pr.at[k], *peers[k]) for k in range(ncol - 1, ncol + 2)
+    ]
     zg = send_z(gy_all, gy_ref, 1)
-    for c in pot_copies:
+    for c in pot_xy:
         c.wait_recv()
 
     eye = (
@@ -267,7 +276,7 @@
     local_x.wait()
 
     def prepare(g):
-        for t in range(group // LANES):
+        def body(t, carry):
             rows = pl.ds(pl.multiple_of(g * group + t * LANES, LANES), LANES)
             xf = x_all[rows, :].astype(jnp.float32)
             sq = jnp.sum(xf * xf, axis=1, keepdims=True) * (1.0 / (2.0 * width))
@@ -278,6 +287,9 @@
             a_lane[0:1, rows] = to_lanes(a)
             b_lane[0:1, rows] = to_lanes(b)
             w_lane[0:1, rows] = to_lanes(w_col[rows, :])
+            return carry
+
+        lax.fori_loop(0, group // LANES, body, 0)
 
     def build(gj, gi):
         down = pl.ds(pl.multiple_of(gj * group, LANES), group)
@@ -305,7 +317,9 @@
 
     prepare(me_r)
     build(me_r, me_r)
-    fw_x = [forward(x_all, 0, k, *xy_x[k]) for k in range(ncol)]
+    fw_x = [forward(x_all, 0, k) for k in range(ncol)]
+    for k in range(ncol):
+        start_forward(xy_x[k], fw_x[k])
     prepare(xn)
     prepare(yn)
 
@@ -326,36 +340,51 @@
     ht_own = nt(gy_all[mine, :], x_all[...])
     ph = pt_own * ht_own
     hc_own = jnp.sum(ph, axis=1, keepdims=True)
-    slot = sums_all.at[me]
+    slot = sums_z.at[me_c]
     slot[:, pl.ds(0, total)] = jnp.sum(fold(ph), axis=0, keepdims=True)
     slot[:, pl.ds(total, LANES)] = jnp.sum(jnp.where(eye, hc_own, 0.0), axis=0, keepdims=True)
-    sum_copies = []
-    for k, (dr, dc) in enumerate(peers):
-        sum_copies.append(
-            copy(slot, slot, hs.at[k], hr_sem.at[k], (me_r + dr) % nrow, (me_c + dc) % ncol)
-        )
+    sum_z = [copy(slot, slot, hs.at[k], hr_sem.at[k], *peers[k]) for k in range(ncol - 1)]
     xy_g = [send_xy(gy_all, gy_ref, 1, 0)]
     for k in range(1, ncol):
         zg[k - 1].wait_recv()
-        xy_g.append(send_xy(gy_all, gy_ref, 1, k))
+        if k < ncol - 1:
+            xy_g.append(send_xy(gy_all, gy_ref, 1, k))
 
     def late(i, carry):
         build(near(jnp.minimum(i, 3)), near(jnp.minimum(6 - i, 3)))
+
+        @pl.when(i == 2)
+        def exchange():
+            for c in sum_z:
+                c.wait_recv()
+            sums_xy[me_r, :, pl.ds(0, total)] = jnp.sum(sums_z[:, :, pl.ds(0, total)], axis=0)
+            for k in range(ncol):
+                sums_xy[me_r, :, pl.ds(total + k * LANES, LANES)] = sums_z[k, :, pl.ds(total, LANES)]
+            for c in sum_xy:
+                c.start()
+
         return carry
 
+    mine_xy = sums_xy.at[me_r]
+    sum_xy = [
+        plan_copy(mine_xy, mine_xy, hs.at[k], hr_sem.at[k], *peers[k]) for k in range(ncol - 1, ncol + 2)
+    ]
     lax.fori_loop(0, 7, late, 0)
-    for c in sum_copies:
+    xy_g.append(send_xy(gy_all, gy_ref, 1, ncol - 1))
+    for c in sum_xy:
         c.wait_recv()
 
     def masses(b, carry):
         rows = pl.ds(pl.multiple_of(b * own, 32), own)
         inv = 1.0 / c_col[rows, :]
         c_col[rows, :] = inv
-        nhc_col[rows, :] = -wide(to_column(sums_all[b, :, pl.ds(total, LANES)])) * inv
+        nhc_col[rows, :] = -wide(
+            to_column(sums_xy[b // ncol, :, pl.ds(pl.multiple_of(total + b % ncol * LANES, LANES), LANES)])
+        ) * inv
         return carry
 
     lax.fori_loop(0, blocks, masses, 0)
-    hr = jnp.sum(sums_all[:, :, pl.ds(0, total)], axis=0)
+    hr = jnp.sum(sums_xy[:, :, pl.ds(0, total)], axis=0)
     inv_r = 1.0 / jnp.sum(r_acc[...], axis=0, keepdims=True)
     phi = -hr * inv_r
     zeros = jnp.zeros((SUBL, total), jnp.float32)
@@ -386,11 +415,19 @@
         acc = lax.fori_loop(0, nrow, body, zeros)
         return -(hr + jnp.sum(acc, axis=0, keepdims=True)) * inv_r
 
-    fw_g = []
-    for step in range(1, ITERS):
+    fw_g = [forward(gy_all, 1, k) for k in range(ncol)]
+
+    def step(i, phi):
         phi = sweep(phi)
-        if step == ITERS - 2:
-            fw_g = [forward(gy_all, 1, k, *xy_g[k]) for k in range(ncol)]
+
+        @pl.when(i == ITERS - 2)
+        def forwards():
+            for k in range(ncol):
+                start_forward(xy_g[k], fw_g[k])
+
+        return phi
+
+    phi = lax.fori_loop(1, ITERS, step, phi)
 
     def last(i, carry):
         psi_of(i, phi)
@@ -424,7 +461,7 @@
     mix = mix + jnp.dot(q_own.astype(jnp.bfloat16), x_all[...], preferred_element_type=jnp.float32)
     gp_ref[...] = (rowterm + (mix - q_sum * x_own.astype(jnp.float32)) * scale).astype(jnp.bfloat16)
 
-    for c in zx + zg + pot_copies + sum_copies:
+    for c in zx + zg + pot_z + pot_xy + sum_z + sum_xy:
         c.wait_send()
     for pairs in (xy_x, fw_x, xy_g, fw_g):
         for one, two in pairs:
@@ -460,15 +497,16 @@
             column, column, column, column, column, column,
             line, line, line,
             pltpu.VMEM((SUBL, total), jnp.float32),
-            pltpu.VMEM((blocks, 1, total + LANES), jnp.float32),
+            pltpu.VMEM((ncol, 1, total + LANES), jnp.float32),
+            pltpu.VMEM((4, 1, total + ncol * LANES), jnp.float32),
             dma((2,)),
             dma((2 * (ncol - 1),)), dma((2 * (ncol - 1),)),
             dma((8 * ncol,)), dma((8 * ncol,)),
-            dma((blocks - 1,)), dma((blocks - 1,)),
-            dma((blocks - 1,)), dma((blocks - 1,)),
+            dma((ncol + 2,)), dma((ncol + 2,)),
+            dma((ncol + 2,)), dma((ncol + 2,)),
         ],
         compiler_params=pltpu.CompilerParams(
-            collective_id=0, has_side_effects=True, vmem_limit_bytes=48 * 1024 * 1024
+            collective_id=0, has_side_effects=True, vmem_limit_bytes=62 * 1024 * 1024
         ),
         cost_estimate=pl.CostEstimate(
             flops=3 * total * total * width, bytes_accessed=4 * own * width, transcendentals=total * total

time: 42.1 us -> 45.5 us (1.081)
  Pallas kernels: 37.8 us -> 41.4 us
  local copies, waits for them, and re-layouts: 3.39 us -> 2.6 us
  other arithmetic: 0.01 us -> 0.6 us
    pallas_call x1, Pallas kernels: 37.8 us -> 41.4 us  [local_fused(): pl.pallas_call(functools.partial(fused_kernel, ncol), out_shape=(jax.Shap...]
    unnamed x12 -> x10, local copies, waits for them, and re-layouts: 3.39 us -> 2.6 us
    another operation x1, other arithmetic: 0.01 us -> 0.6 us  [local_fused(): jnp.stack([row_potential, col_potential, weights])]
where the time goes in v3:
time: 45.5 us; the launch traced here: 45.2 us
  Pallas kernels  41.4 us (91%)
  local copies, waits for them, and re-layouts  2.6 us (6%)
  between operations  0.67 us (1%)
  other arithmetic  0.6 us (1%)
    pallas_call x1, Pallas kernels, local_fused(): pl.pallas_call(functools.partial(fused_kernel, ncol), out_shape=(jax.Shap...  41.4 us
    unnamed x10, local copies, waits for them, and re-layouts  2.6 us

profile of v3, /device:TPU:0, one launch (start us, length us, event | category | flops | bytes accessed | tf_op | source)
XLA Modules:
  0.0 45.2 jit_solution(7507299071185021879)
XLA Ops:
  0.6 0.0 copy-start
  0.6 0.0 copy-start.1
  0.7 0.0 copy-start.2
  0.7 0.6 %copy-done = bf16[96]{0:T(256)(128)(2,1)S(1)} copy-done((bf16[96]{0:T(256)(128)(2,1)S(1)}, bf16[96]{0:T(256)(128)(2,1)}, u32[]{:S(2)}) %copy-start) | copy-done | bytes 216
  1.3 0.0 copy-done.1
  1.3 0.0 copy-done.2
  1.3 0.6 %fusion.8.pot_ref = bf16[16,128]{1,0:T(8,128)(2,1)} fusion(bf16[1,96]{1,0:T(2,128)(2,1)S(1)} %bitcast.4, bf16[1,96]{1,0:T(2,128)(2,1)S(1)} %bitcast.5, bf16[1,96]{1,0:T(2,128)(2,1)S(1)} %bitcast.6), kind=kLoop, calls=%fused_computation.10 | loop fusion | flops 30720 | bytes 4672 | tf_op jit(solution)/shard_map/stack | solution.py:477
  1.9 41.4 %shard_map.68 = (bf16[96,256]{1,0:T(8,128)(2,1)}, f32[1,96]{1,0:T(1,128)}) custom-call(bf16[96,256]{1,0:T(8,128)(2,1)} %x_ref.1, bf16[96,256]{1,0:T(8,128)(2,1)} %gy_ref.1, bf16[16,128]{1,0:T(8,128)(2,1)} %fusion.8.pot_ref), custom_call_target="tpu_custom_call" | custom-call | flops 1811939328 | bytes 98304 | tf_op jit(solution)/shard_map/pallas_call | solution.py:484
  43.3 0.0 copy-start.3
  43.3 1.4 %copy.9 = bf16[96,256]{1,0:T(8,128)(2,1)} copy(bf16[96,256]{1,0:T(8,128)(2,1)} %get-tuple-element.8) | data formatting | bytes 98304
  44.7 0.0 copy-done.3
  44.7 0.5 %copy.10 = f32[96]{0:T(128)} copy(f32[96]{0:T(128)S(1)} %bitcast.7) | data formatting | bytes 768
Async XLA Ops:
  0.6 0.7 %copy-start = (bf16[96]{0:T(256)(128)(2,1)S(1)}, bf16[96]{0:T(256)(128)(2,1)}, u32[]{:S(2)}) copy-start(bf16[96]{0:T(256)(128)(2,1)} %param.9) | copy-start | bytes 580
  0.6 0.7 %copy-start.1 = (bf16[96]{0:T(256)(128)(2,1)S(1)}, bf16[96]{0:T(256)(128)(2,1)}, u32[]{:S(2)}) copy-start(bf16[96]{0:T(256)(128)(2,1)} %param.8) | copy-start | bytes 580
  0.7 0.7 %copy-start.2 = (bf16[96]{0:T(256)(128)(2,1)S(1)}, bf16[96]{0:T(256)(128)(2,1)}, u32[]{:S(2)}) copy-start(bf16[96]{0:T(256)(128)(2,1)} %param.7) | copy-start | bytes 580
  43.3 1.4 %copy-start.3 = (f32[1,96]{1,0:T(1,128)S(1)}, f32[1,96]{1,0:T(1,128)}, u32[]{:S(2)}) copy-start(f32[1,96]{1,0:T(1,128)} %get-tuple-element.5) | copy-start | bytes 1156

commit v4 on v2

--- a/solution.py
+++ b/solution.py
@@ -144,15 +144,17 @@
 
 
 def fused_kernel(
-    ncol, x_ref, gy_ref, pot_ref, gp_ref, gw_ref,
+    ncol, own, pack_ref, gp_ref, gw_ref,
     x_all, gy_all, pots, plan, a_col, b_col, w_col, c_col, nhc_col, psi_col,
     a_lane, b_lane, w_lane, r_acc, sums_all,
     ls, zs, zr, xs, xr, ps, pr, hs, hr_sem,
 ):
     nrow = 4
-    own = x_ref.shape[0]
     half = own // 2
-    width = x_ref.shape[1]
+    width = pack_ref.shape[1]
+    x_ref = pack_ref.at[pl.ds(0, own)]
+    gy_ref = pack_ref.at[pl.ds(own, own)]
+    pot_ref = pack_ref.at[pl.ds(2 * own, 16), pl.ds(0, LANES)]
     blocks = nrow * ncol
     total = own * blocks
     group = own * ncol
@@ -163,7 +165,9 @@
     xn = me_r + 1 - 2 * (me_r % 2)
     yn = (me_r + 2) % nrow
     dn = (xn + 2) % nrow
-    peers = [(dr, dc) for dr in range(nrow) for dc in range(ncol) if dr or dc]
+    peers = [
+        ((me_r + dr) % nrow, (me_c + dc) % ncol) for dr in range(nrow) for dc in range(ncol) if dr or dc
+    ]
     scale = 1.0 / (width * EPS)
 
     def at(row, col, part=None):
@@ -181,10 +185,9 @@
     local_g = pltpu.make_async_copy(gy_ref, gy_all.at[mine], ls.at[1])
     local_g.start()
     barrier = pltpu.get_barrier_semaphore()
-    for dr, dc in peers:
+    for row, col in peers:
         pl.semaphore_signal(
-            barrier, inc=1, device_id=dev((me_r + dr) % nrow, (me_c + dc) % ncol),
-            device_id_type=pl.DeviceIdType.MESH,
+            barrier, inc=1, device_id=dev(row, col), device_id_type=pl.DeviceIdType.MESH
         )
     my_pot = pl.ds(pl.multiple_of(me * 16, 16), 16)
     pots[my_pot, :] = pot_ref[...]
@@ -192,11 +195,14 @@
     c_col[...] = jnp.zeros_like(c_col)
     pl.semaphore_wait(barrier, len(peers))
 
-    def copy(src, dst, ssem, rsem, row, col):
-        c = pltpu.make_async_remote_copy(
+    def plan_copy(src, dst, ssem, rsem, row, col):
+        return pltpu.make_async_remote_copy(
             src_ref=src, dst_ref=dst, send_sem=ssem, recv_sem=rsem,
             device_id=dev(row, col), device_id_type=pl.DeviceIdType.MESH,
         )
+
+    def copy(*args):
+        c = plan_copy(*args)
         c.start()
         return c
 
@@ -207,37 +213,42 @@
             out.append(copy(ref, buf.at[mine], zs.at[k], zr.at[k], me_r, (me_c + dc) % ncol))
         return out
 
-    def send_xy(buf, ref, n, k):
-        here = buf.at[at(me_r, (me_c + ncol - k) % ncol)]
+    def send_plane(buf, ref, n, k):
+        col = (me_c + ncol - k) % ncol
+        here = buf.at[at(me_r, col)]
         src = ref if k == 0 else here
-        s = (n * ncol + k) * 4
-        return (
+        s = (n * ncol + k) * 3
+        out = [
             copy(src, here, xs.at[s], xr.at[s], xn, me_c),
             copy(src, here, xs.at[s + 1], xr.at[s + 1], yn, me_c),
-        )
-
-    def forward(buf, n, k, first, second):
-        col = (me_c + ncol - k) % ncol
-        s = (n * ncol + k) * 4
-        first.wait_recv()
-        src = buf.at[at(xn, col, 0)]
-        one = copy(src, src, xs.at[s + 2], xr.at[s + 2], yn, me_c)
-        second.wait_recv()
-        src = buf.at[at(yn, col, 1)]
-        two = copy(src, src, xs.at[s + 3], xr.at[s + 3], xn, me_c)
-        return (one, two)
+        ]
+        if k == 0:
+            out.append(copy(src, here, xs.at[s + 2], xr.at[s + 2], dn, me_c))
+        else:
+            here = buf.at[at(me_r, col, 0)]
+            out.append(copy(here, here, xs.at[s + 2], xr.at[s + 2], dn, me_c))
+        return out
+
+    def relay(buf, n, came):
+        came.wait_recv()
+        here = buf.at[at(dn, me_c, 1)]
+        out = []
+        for dc in range(1, ncol):
+            k = (2 + n) * (ncol - 1) + dc - 1
+            out.append(copy(here, here, zs.at[k], zr.at[k], me_r, (me_c + dc) % ncol))
+        return out
 
     zx = send_z(x_all, x_ref, 0)
-    xy_x = [send_xy(x_all, x_ref, 0, 0)]
-    pot_copies = []
-    for k, (dr, dc) in enumerate(peers):
-        pot_copies.append(
-            copy(pot_ref, pots.at[my_pot], ps.at[k], pr.at[k], (me_r + dr) % nrow, (me_c + dc) % ncol)
-        )
+    plane_x = [send_plane(x_all, x_ref, 0, 0)]
+    pot_copies = [
+        copy(pot_ref, pots.at[my_pot], ps.at[k], pr.at[k], *peers[k]) for k in range(len(peers))
+    ]
     for k in range(1, ncol):
         zx[k - 1].wait_recv()
-        xy_x.append(send_xy(x_all, x_ref, 0, k))
+        plane_x.append(send_plane(x_all, x_ref, 0, k))
+    zx += relay(x_all, 0, plane_x[0][2])
     zg = send_z(gy_all, gy_ref, 1)
+    plane_g = [send_plane(gy_all, gy_ref, 1, 0)]
     for c in pot_copies:
         c.wait_recv()
 
@@ -267,7 +278,7 @@
     local_x.wait()
 
     def prepare(g):
-        for t in range(group // LANES):
+        def body(t, carry):
             rows = pl.ds(pl.multiple_of(g * group + t * LANES, LANES), LANES)
             xf = x_all[rows, :].astype(jnp.float32)
             sq = jnp.sum(xf * xf, axis=1, keepdims=True) * (1.0 / (2.0 * width))
@@ -278,6 +289,9 @@
             a_lane[0:1, rows] = to_lanes(a)
             b_lane[0:1, rows] = to_lanes(b)
             w_lane[0:1, rows] = to_lanes(w_col[rows, :])
+            return carry
+
+        lax.fori_loop(0, group // LANES, body, 0)
 
     def build(gj, gi):
         down = pl.ds(pl.multiple_of(gj * group, LANES), group)
@@ -305,8 +319,11 @@
 
     prepare(me_r)
     build(me_r, me_r)
-    fw_x = [forward(x_all, 0, k, *xy_x[k]) for k in range(ncol)]
+    for sent in plane_x:
+        sent[0].wait_recv()
     prepare(xn)
+    for sent in plane_x:
+        sent[1].wait_recv()
     prepare(yn)
 
     def early(i, carry):
@@ -314,9 +331,10 @@
         return carry
 
     lax.fori_loop(1, 9, early, 0)
-    for one, two in fw_x:
-        one.wait_recv()
-        two.wait_recv()
+    for sent in plane_x[1:]:
+        sent[2].wait_recv()
+    for c in zx[ncol - 1 :]:
+        c.wait_recv()
     prepare(dn)
 
     x_own = x_all[mine, :]
@@ -329,15 +347,9 @@
     slot = sums_all.at[me]
     slot[:, pl.ds(0, total)] = jnp.sum(fold(ph), axis=0, keepdims=True)
     slot[:, pl.ds(total, LANES)] = jnp.sum(jnp.where(eye, hc_own, 0.0), axis=0, keepdims=True)
-    sum_copies = []
-    for k, (dr, dc) in enumerate(peers):
-        sum_copies.append(
-            copy(slot, slot, hs.at[k], hr_sem.at[k], (me_r + dr) % nrow, (me_c + dc) % ncol)
-        )
-    xy_g = [send_xy(gy_all, gy_ref, 1, 0)]
-    for k in range(1, ncol):
-        zg[k - 1].wait_recv()
-        xy_g.append(send_xy(gy_all, gy_ref, 1, k))
+    sum_copies = [
+        copy(slot, slot, hs.at[k], hr_sem.at[k], *peers[k]) for k in range(len(peers))
+    ]
 
     def late(i, carry):
         build(near(jnp.minimum(i, 3)), near(jnp.minimum(6 - i, 3)))
@@ -346,6 +358,10 @@
     lax.fori_loop(0, 7, late, 0)
     for c in sum_copies:
         c.wait_recv()
+    for k in range(1, ncol):
+        zg[k - 1].wait_recv()
+        plane_g.append(send_plane(gy_all, gy_ref, 1, k))
+    zg += relay(gy_all, 1, plane_g[0][2])
 
     def masses(b, carry):
         rows = pl.ds(pl.multiple_of(b * own, 32), own)
@@ -386,11 +402,7 @@
         acc = lax.fori_loop(0, nrow, body, zeros)
         return -(hr + jnp.sum(acc, axis=0, keepdims=True)) * inv_r
 
-    fw_g = []
-    for step in range(1, ITERS):
-        phi = sweep(phi)
-        if step == ITERS - 2:
-            fw_g = [forward(gy_all, 1, k, *xy_g[k]) for k in range(ncol)]
+    phi = lax.fori_loop(1, ITERS, lambda i, line: sweep(line), phi)
 
     def last(i, carry):
         psi_of(i, phi)
@@ -415,9 +427,13 @@
     phi_row = jnp.sum(jnp.where(eye, phi_own, 0.0), axis=0, keepdims=True)
     gw_ref[...] = (-(total / w_sum) * (phi_row - w_phi / w_sum))[:, :own]
 
-    for one, two in fw_g:
-        one.wait_recv()
-        two.wait_recv()
+    for k in range(ncol):
+        plane_g[k][0].wait_recv()
+        plane_g[k][1].wait_recv()
+        if k:
+            plane_g[k][2].wait_recv()
+    for c in zg[ncol - 1 :]:
+        c.wait_recv()
     q_own = p_own * (nt(x_own, gy_all[...]) + (phi_own + psi_lane))
     q_sum = jnp.sum(q_own, axis=1, keepdims=True)
     rowterm = jnp.dot(p_own.astype(jnp.bfloat16), gy_all[...], preferred_element_type=jnp.float32)
@@ -426,10 +442,9 @@
 
     for c in zx + zg + pot_copies + sum_copies:
         c.wait_send()
-    for pairs in (xy_x, fw_x, xy_g, fw_g):
-        for one, two in pairs:
-            one.wait_send()
-            two.wait_send()
+    for sent in plane_x + plane_g:
+        for c in sent:
+            c.wait_send()
 
 
 def local_fused(ncol, particles, cotangent, row_potential, col_potential, weights):
@@ -437,20 +452,20 @@
     blocks = 4 * ncol
     total = own * blocks
     pot = jnp.pad(
-        jnp.stack([row_potential, col_potential, weights]), ((0, 13), (0, LANES - own))
-    )
+        jnp.stack([row_potential, col_potential, weights]), ((0, 13), (0, width - own))
+    )
+    pack = jnp.concatenate([particles, cotangent, pot], axis=0)
     column = pltpu.VMEM((total, LANES), jnp.float32)
     line = pltpu.VMEM((1, total), jnp.float32)
     dma = pltpu.SemaphoreType.DMA
     vmem = pl.BlockSpec(memory_space=pltpu.VMEM)
-    hbm = pl.BlockSpec(memory_space=pltpu.HBM)
     gp, gw = pl.pallas_call(
-        functools.partial(fused_kernel, ncol),
+        functools.partial(fused_kernel, ncol, own),
         out_shape=(
             jax.ShapeDtypeStruct((own, width), jnp.bfloat16),
             jax.ShapeDtypeStruct((1, own), jnp.float32),
         ),
-        in_specs=[hbm, hbm, vmem],
+        in_specs=[vmem],
         out_specs=[vmem, vmem],
         scratch_shapes=[
             pltpu.VMEM((total, width), jnp.bfloat16),
@@ -462,8 +477,8 @@
             pltpu.VMEM((SUBL, total), jnp.float32),
             pltpu.VMEM((blocks, 1, total + LANES), jnp.float32),
             dma((2,)),
-            dma((2 * (ncol - 1),)), dma((2 * (ncol - 1),)),
-            dma((8 * ncol,)), dma((8 * ncol,)),
+            dma((4 * (ncol - 1),)), dma((4 * (ncol - 1),)),
+            dma((6 * ncol,)), dma((6 * ncol,)),
             dma((blocks - 1,)), dma((blocks - 1,)),
             dma((blocks - 1,)), dma((blocks - 1,)),
         ],
@@ -473,7 +488,7 @@
         cost_estimate=pl.CostEstimate(
             flops=3 * total * total * width, bytes_accessed=4 * own * width, transcendentals=total * total
         ),
-    )(particles, cotangent, pot)
+    )(pack)
     return gp, gw.reshape(own)
 
 

time: 42.1 us -> 40 us (0.950)
  local copies, waits for them, and re-layouts: 3.39 us -> 1.8 us
  Pallas kernels: 37.8 us -> 36.5 us
  other arithmetic: 0.01 us -> 0.84 us
    unnamed x12 -> x8, local copies, waits for them, and re-layouts: 3.39 us -> 1.8 us
    pallas_call x1, Pallas kernels: 37.8 us -> 36.5 us  [local_fused(): pl.pallas_call(functools.partial(fused_kernel, ncol, own), out_shape=(jax...]
    concatenate x0 -> x1, other arithmetic: none -> 0.83 us  [local_fused(): pack = jnp.concatenate([particles, cotangent, pot], axis=0)]
where the time goes in v4:
time: 40 us; the launch traced here: 39.8 us
  Pallas kernels  36.5 us (91%)
  local copies, waits for them, and re-layouts  1.8 us (4%)
  other arithmetic  0.84 us (2%)
  between operations  0.67 us (2%)
    pallas_call x1, Pallas kernels, local_fused(): pl.pallas_call(functools.partial(fused_kernel, ncol, own), out_shape=(jax...  36.5 us
    unnamed x8, local copies, waits for them, and re-layouts  1.8 us
    concatenate x1, other arithmetic, local_fused(): pack = jnp.concatenate([particles, cotangent, pot], axis=0)  0.83 us

profile of v4, /device:TPU:0, one launch (start us, length us, event | category | flops | bytes accessed | tf_op | source)
XLA Modules:
  0.0 39.8 jit_solution(8041015577935866010)
XLA Ops:
  0.6 0.0 copy-start
  0.6 0.0 copy-start.1
  0.7 0.0 copy-start.2
  0.7 0.6 %copy-done = bf16[96]{0:T(256)(128)(2,1)S(1)} copy-done((bf16[96]{0:T(256)(128)(2,1)S(1)}, bf16[96]{0:T(256)(128)(2,1)}, u32[]{:S(2)}) %copy-start) | copy-done | bytes 216
  1.3 0.0 copy-done.1
  1.3 0.0 copy-done.2
  1.3 0.8 %pad_maximum_fusion.pack_ref = bf16[208,256]{1,0:T(8,128)(2,1)S(1)} fusion(bf16[16,256]{1,0:T(8,128)(2,1)S(1)} %fusion.8, bf16[96,256]{1,0:T(8,128)(2,1)} %param.6, bf16[96,256]{1,0:T(8,128)(2,1)} %param.5), kind=kLoop, calls=%fused_computation | loop fusion | flops 319488 | bytes 212992 | tf_op jit(solution)/shard_map/concatenate | solution.py:457
  2.2 36.5 %shard_map.68 = (bf16[96,256]{1,0:T(8,128)(2,1)S(1)}, f32[1,96]{1,0:T(1,128)S(1)}) custom-call(bf16[208,256]{1,0:T(8,128)(2,1)S(1)} %pad_maximum_fusion.pack_ref), custom_call_target="tpu_custom_call" | custom-call | flops 1811939328 | bytes 98304 | tf_op jit(solution)/shard_map/pallas_call | solution.py:462
  38.7 0.6 %copy.9 = bf16[96,256]{1,0:T(8,128)(2,1)} copy(bf16[96,256]{1,0:T(8,128)(2,1)S(1)} %get-tuple-element.8) | data formatting | bytes 98304
  39.3 0.5 %copy.10 = f32[96]{0:T(128)} copy(f32[96]{0:T(128)S(1)} %bitcast.4) | data formatting | bytes 768
  (1 shorter events, 0.0 us)
Async XLA Ops:
  0.6 0.7 %copy-start = (bf16[96]{0:T(256)(128)(2,1)S(1)}, bf16[96]{0:T(256)(128)(2,1)}, u32[]{:S(2)}) copy-start(bf16[96]{0:T(256)(128)(2,1)} %param.9) | copy-start | bytes 580
  0.6 0.7 %copy-start.1 = (bf16[96]{0:T(256)(128)(2,1)S(1)}, bf16[96]{0:T(256)(128)(2,1)}, u32[]{:S(2)}) copy-start(bf16[96]{0:T(256)(128)(2,1)} %param.8) | copy-start | bytes 580
  0.7 0.7 %copy-start.2 = (bf16[96]{0:T(256)(128)(2,1)S(1)}, bf16[96]{0:T(256)(128)(2,1)}, u32[]{:S(2)}) copy-start(bf16[96]{0:T(256)(128)(2,1)} %param.7) | copy-start | bytes 580

commit v5 on v4

--- a/solution.py
+++ b/solution.py
@@ -137,6 +137,14 @@
     return jnp.broadcast_to(column, (column.shape[0], LANES))
 
 
+def lane_sums(parts):
+    high = parts.astype(jnp.bfloat16)
+    low = (parts - high.astype(jnp.float32)).astype(jnp.bfloat16)
+    both = jnp.concatenate([high, low], axis=1)
+    ones = jnp.ones((both.shape[1], LANES), jnp.bfloat16)
+    return jnp.dot(both, ones, preferred_element_type=jnp.float32)
+
+
 def nt(left, right):
     return lax.dot_general(
         left, right, (((1,), (1,)), ((), ())), preferred_element_type=jnp.float32
@@ -145,7 +153,7 @@
 
 def fused_kernel(
     ncol, own, pack_ref, gp_ref, gw_ref,
-    x_all, gy_all, pots, plan, a_col, b_col, w_col, c_col, nhc_col, psi_col,
+    x_all, gy_all, pots, plan, a_col, b_col, c_col, nhc_col, psi_col,
     a_lane, b_lane, w_lane, r_acc, sums_all,
     ls, zs, zr, xs, xr, ps, pr, hs, hr_sem,
 ):
@@ -264,34 +272,36 @@
     def to_lanes(column):
         return jnp.sum(jnp.where(eye_l, column, 0.0), axis=0, keepdims=True)
 
-    def to_column(line):
-        return jnp.sum(jnp.where(eye, jnp.broadcast_to(line, (own, LANES)), 0.0), axis=1, keepdims=True)
-
-    def spread(b, carry):
-        rows = pl.ds(pl.multiple_of(b * own, 32), own)
-        pot = pots[pl.ds(pl.multiple_of(b * 16, 16), 16), :].astype(jnp.float32)
-        for k, dst in ((0, a_col), (1, b_col), (2, w_col)):
-            dst[rows, :] = wide(to_column(pot[k : k + 1, :]))
-        return carry
-
-    lax.fori_loop(0, blocks, spread, 0)
+    def on_diagonal(lines):
+        spots = [jnp.where(eye, jnp.broadcast_to(line, (own, LANES)), 0.0) for line in lines]
+        return jnp.concatenate(spots, axis=0)
+
+    ones = jnp.ones((LANES, LANES), jnp.bfloat16)
     local_x.wait()
 
     def prepare(g):
-        def body(t, carry):
-            rows = pl.ds(pl.multiple_of(g * group + t * LANES, LANES), LANES)
-            xf = x_all[rows, :].astype(jnp.float32)
-            sq = jnp.sum(xf * xf, axis=1, keepdims=True) * (1.0 / (2.0 * width))
-            a = (a_col[rows, :] - sq) * (1.0 / EPS)
-            b = (b_col[rows, :] - sq) * (1.0 / EPS)
-            a_col[rows, :] = a
-            b_col[rows, :] = b
-            a_lane[0:1, rows] = to_lanes(a)
-            b_lane[0:1, rows] = to_lanes(b)
-            w_lane[0:1, rows] = to_lanes(w_col[rows, :])
-            return carry
-
-        lax.fori_loop(0, group // LANES, body, 0)
+        rows = pl.ds(pl.multiple_of(g * group, LANES), group)
+        pot = pots[pl.ds(pl.multiple_of(g * 16 * ncol, 16), 16 * ncol), :].astype(jnp.float32)
+        f, gp, w = [
+            jnp.dot(
+                on_diagonal([pot[16 * b + k : 16 * b + k + 1, :] for b in range(ncol)]).astype(jnp.bfloat16),
+                ones,
+                preferred_element_type=jnp.float32,
+            )
+            for k in range(3)
+        ]
+        xf = x_all[rows, :].astype(jnp.float32)
+        sq = lane_sums(xf * xf) * (1.0 / (2.0 * width))
+        a = (f - sq) * (1.0 / EPS)
+        b = (gp - sq) * (1.0 / EPS)
+        a_col[rows, :] = a
+        b_col[rows, :] = b
+        for t in range(group // LANES):
+            lanes = pl.ds(pl.multiple_of(g * group + t * LANES, LANES), LANES)
+            here = slice(t * LANES, (t + 1) * LANES)
+            a_lane[0:1, lanes] = to_lanes(a[here])
+            b_lane[0:1, lanes] = to_lanes(b[here])
+            w_lane[0:1, lanes] = to_lanes(w[here])
 
     def build(gj, gi):
         down = pl.ds(pl.multiple_of(gj * group, LANES), group)
@@ -309,7 +319,7 @@
                 plan[rows, lanes] = p
                 part = part + p
                 accs[t] = accs[t] + fold(p)
-            c_col[rows, :] += wide(jnp.sum(part, axis=1, keepdims=True))
+            c_col[rows, :] += part
         for t in range(group // LANES):
             lanes = pl.ds(pl.multiple_of(gi * group + t * LANES, LANES), LANES)
             r_acc[:, lanes] += accs[t]
@@ -363,52 +373,54 @@
         plane_g.append(send_plane(gy_all, gy_ref, 1, k))
     zg += relay(gy_all, 1, plane_g[0][2])
 
-    def masses(b, carry):
-        rows = pl.ds(pl.multiple_of(b * own, 32), own)
-        inv = 1.0 / c_col[rows, :]
+    for g in range(nrow):
+        rows = pl.ds(g * group, group)
+        inv = 1.0 / lane_sums(c_col[rows, :])
         c_col[rows, :] = inv
-        nhc_col[rows, :] = -wide(to_column(sums_all[b, :, pl.ds(total, LANES)])) * inv
-        return carry
-
-    lax.fori_loop(0, blocks, masses, 0)
+        lines = [sums_all[g * ncol + b, :, pl.ds(total, LANES)] for b in range(ncol)]
+        nhc_col[rows, :] = -lane_sums(on_diagonal(lines)) * inv
     hr = jnp.sum(sums_all[:, :, pl.ds(0, total)], axis=0)
     inv_r = 1.0 / jnp.sum(r_acc[...], axis=0, keepdims=True)
     phi = -hr * inv_r
-    zeros = jnp.zeros((SUBL, total), jnp.float32)
 
     def cut(value, t):
         return value[:, t * LANES : (t + 1) * LANES]
 
-    def psi_of(i, phi):
+    def psi_of(g, phi):
+        phi8 = jnp.broadcast_to(phi, (SUBL, total))
+        parts = []
         for s in range(group // SUB):
-            rows = pl.ds(pl.multiple_of(i * group + s * SUB, SUB), SUB)
-            part = plan[rows, pl.ds(0, LANES)] * cut(phi, 0)
-            for t in range(1, tiles):
-                part = part + plan[rows, pl.ds(t * LANES, LANES)] * cut(phi, t)
-            total_s = wide(jnp.sum(part, axis=1, keepdims=True))
-            psi_col[rows, :] = nhc_col[rows, :] - total_s * c_col[rows, :]
-
-    def sweep(phi):
-        def body(i, acc):
-            psi_of(i, phi)
-            accs = [cut(acc, t) for t in range(tiles)]
-            for s in range(group // SUB):
-                rows = pl.ds(pl.multiple_of(i * group + s * SUB, SUB), SUB)
-                psi = psi_col[rows, :]
-                for t in range(tiles):
-                    accs[t] = accs[t] + fold(plan[rows, pl.ds(t * LANES, LANES)] * psi)
-            return jnp.concatenate(accs, axis=1)
-
-        acc = lax.fori_loop(0, nrow, body, zeros)
-        return -(hr + jnp.sum(acc, axis=0, keepdims=True)) * inv_r
-
-    phi = lax.fori_loop(1, ITERS, lambda i, line: sweep(line), phi)
-
-    def last(i, carry):
-        psi_of(i, phi)
-        return carry
-
-    lax.fori_loop(0, nrow, last, 0)
+            rows = pl.ds(pl.multiple_of(g * group + s * SUB, SUB), SUB)
+            part = jnp.zeros((SUB // SUBL, SUBL, LANES), jnp.float32)
+            for t in range(tiles):
+                piece = plan[rows, pl.ds(t * LANES, LANES)].reshape(SUB // SUBL, SUBL, LANES)
+                part = part + piece * cut(phi8, t)[None]
+            parts.append(part.reshape(SUB, LANES))
+        rows = pl.ds(pl.multiple_of(g * group, LANES), group)
+        return nhc_col[rows, :] - lane_sums(jnp.concatenate(parts, axis=0)) * c_col[rows, :]
+
+    def add_columns(g, psi, accs):
+        out = list(accs)
+        for s in range(group // SUB):
+            rows = pl.ds(g * group + s * SUB, SUB)
+            here = psi[s * SUB : (s + 1) * SUB]
+            for t in range(tiles):
+                out[t] = out[t] + fold(plan[rows, pl.ds(t * LANES, LANES)] * here)
+        return out
+
+    def sweep(i, phi):
+        accs = [jnp.zeros((SUBL, LANES), jnp.float32)] * tiles
+        psi = psi_of(0, phi)
+        for g in range(1, nrow):
+            later = psi_of(g, phi)
+            accs = add_columns(g - 1, psi, accs)
+            psi = later
+        accs = add_columns(nrow - 1, psi, accs)
+        return -(hr + jnp.sum(jnp.concatenate(accs, axis=1), axis=0, keepdims=True)) * inv_r
+
+    phi = lax.fori_loop(1, ITERS, sweep, phi)
+    for g in range(nrow):
+        psi_col[pl.ds(g * group, group), :] = psi_of(g, phi)
     psi_lane = jnp.concatenate(
         [to_lanes(psi_col[pl.ds(t * LANES, LANES), :]) for t in range(tiles)], axis=1
     )
@@ -472,7 +484,7 @@
             pltpu.VMEM((total, width), jnp.bfloat16),
             pltpu.VMEM((16 * blocks, LANES), jnp.bfloat16),
             pltpu.VMEM((total, total), jnp.float32),
-            column, column, column, column, column, column,
+            column, column, column, column, column,
             line, line, line,
             pltpu.VMEM((SUBL, total), jnp.float32),
             pltpu.VMEM((blocks, 1, total + LANES), jnp.float32),

time: 40 us -> 38.9 us (0.972)
  Pallas kernels: 36.5 us -> 35.4 us
    pallas_call x1, Pallas kernels: 36.5 us -> 35.4 us  [local_fused(): pl.pallas_call(functools.partial(fused_kernel, ncol, own), out_shape=(jax...]
where the time goes in v5:
time: 38.9 us; the launch traced here: 38.7 us
  Pallas kernels  35.4 us (91%)
  local copies, waits for them, and re-layouts  1.8 us (5%)
  other arithmetic  0.84 us (2%)
  between operations  0.67 us (2%)
    pallas_call x1, Pallas kernels, local_fused(): pl.pallas_call(functools.partial(fused_kernel, ncol, own), out_shape=(jax...  35.4 us
    unnamed x8, local copies, waits for them, and re-layouts  1.8 us
    concatenate x1, other arithmetic, local_fused(): pack = jnp.concatenate([particles, cotangent, pot], axis=0)  0.83 us

profile of v5, /device:TPU:0, one launch (start us, length us, event | category | flops | bytes accessed | tf_op | source)
XLA Modules:
  0.0 38.7 jit_solution(16536869215144701885)
XLA Ops:
  0.6 0.0 copy-start
  0.6 0.0 copy-start.1
  0.7 0.0 copy-start.2
  0.7 0.6 %copy-done = bf16[96]{0:T(256)(128)(2,1)S(1)} copy-done((bf16[96]{0:T(256)(128)(2,1)S(1)}, bf16[96]{0:T(256)(128)(2,1)}, u32[]{:S(2)}) %copy-start) | copy-done | bytes 216
  1.3 0.0 copy-done.1
  1.3 0.0 copy-done.2
  1.3 0.8 %pad_maximum_fusion.pack_ref = bf16[208,256]{1,0:T(8,128)(2,1)S(1)} fusion(bf16[16,256]{1,0:T(8,128)(2,1)S(1)} %fusion.8, bf16[96,256]{1,0:T(8,128)(2,1)} %param.6, bf16[96,256]{1,0:T(8,128)(2,1)} %param.5), kind=kLoop, calls=%fused_computation | loop fusion | flops 319488 | bytes 212992 | tf_op jit(solution)/shard_map/concatenate | solution.py:469
  2.2 35.4 %shard_map.68 = (bf16[96,256]{1,0:T(8,128)(2,1)S(1)}, f32[1,96]{1,0:T(1,128)S(1)}) custom-call(bf16[208,256]{1,0:T(8,128)(2,1)S(1)} %pad_maximum_fusion.pack_ref), custom_call_target="tpu_custom_call" | custom-call | flops 1811939328 | bytes 98304 | tf_op jit(solution)/shard_map/pallas_call | solution.py:474
  37.6 0.6 %copy.9 = bf16[96,256]{1,0:T(8,128)(2,1)} copy(bf16[96,256]{1,0:T(8,128)(2,1)S(1)} %get-tuple-element.8) | data formatting | bytes 98304
  38.2 0.5 %copy.10 = f32[96]{0:T(128)} copy(f32[96]{0:T(128)S(1)} %bitcast.4) | data formatting | bytes 768
  (1 shorter events, 0.0 us)
Async XLA Ops:
  0.6 0.7 %copy-start = (bf16[96]{0:T(256)(128)(2,1)S(1)}, bf16[96]{0:T(256)(128)(2,1)}, u32[]{:S(2)}) copy-start(bf16[96]{0:T(256)(128)(2,1)} %param.9) | copy-start | bytes 580
  0.6 0.7 %copy-start.1 = (bf16[96]{0:T(256)(128)(2,1)S(1)}, bf16[96]{0:T(256)(128)(2,1)}, u32[]{:S(2)}) copy-start(bf16[96]{0:T(256)(128)(2,1)} %param.8) | copy-start | bytes 580
  0.7 0.7 %copy-start.2 = (bf16[96]{0:T(256)(128)(2,1)S(1)}, bf16[96]{0:T(256)(128)(2,1)}, u32[]{:S(2)}) copy-start(bf16[96]{0:T(256)(128)(2,1)} %param.7) | copy-start | bytes 580

commit v6 on v5

--- a/solution.py
+++ b/solution.py
@@ -133,10 +133,6 @@
     return jnp.sum(block.reshape(block.shape[0] // SUBL, SUBL, block.shape[1]), axis=0)
 
 
-def wide(column):
-    return jnp.broadcast_to(column, (column.shape[0], LANES))
-
-
 def lane_sums(parts):
     high = parts.astype(jnp.bfloat16)
     low = (parts - high.astype(jnp.float32)).astype(jnp.bfloat16)
@@ -152,7 +148,7 @@
 
 
 def fused_kernel(
-    ncol, own, pack_ref, gp_ref, gw_ref,
+    ncol, own, pack_ref, pot_ref, gp_ref, gw_ref,
     x_all, gy_all, pots, plan, a_col, b_col, c_col, nhc_col, psi_col,
     a_lane, b_lane, w_lane, r_acc, sums_all,
     ls, zs, zr, xs, xr, ps, pr, hs, hr_sem,
@@ -162,7 +158,6 @@
     width = pack_ref.shape[1]
     x_ref = pack_ref.at[pl.ds(0, own)]
     gy_ref = pack_ref.at[pl.ds(own, own)]
-    pot_ref = pack_ref.at[pl.ds(2 * own, 16), pl.ds(0, LANES)]
     blocks = nrow * ncol
     total = own * blocks
     group = own * ncol
@@ -197,8 +192,7 @@
         pl.semaphore_signal(
             barrier, inc=1, device_id=dev(row, col), device_id_type=pl.DeviceIdType.MESH
         )
-    my_pot = pl.ds(pl.multiple_of(me * 16, 16), 16)
-    pots[my_pot, :] = pot_ref[...]
+    pots[me, :, :] = pot_ref[...]
     r_acc[...] = jnp.zeros_like(r_acc)
     c_col[...] = jnp.zeros_like(c_col)
     pl.semaphore_wait(barrier, len(peers))
@@ -249,14 +243,12 @@
     zx = send_z(x_all, x_ref, 0)
     plane_x = [send_plane(x_all, x_ref, 0, 0)]
     pot_copies = [
-        copy(pot_ref, pots.at[my_pot], ps.at[k], pr.at[k], *peers[k]) for k in range(len(peers))
+        copy(pot_ref, pots.at[me], ps.at[k], pr.at[k], *peers[k]) for k in range(len(peers))
     ]
     for k in range(1, ncol):
         zx[k - 1].wait_recv()
         plane_x.append(send_plane(x_all, x_ref, 0, k))
     zx += relay(x_all, 0, plane_x[0][2])
-    zg = send_z(gy_all, gy_ref, 1)
-    plane_g = [send_plane(gy_all, gy_ref, 1, 0)]
     for c in pot_copies:
         c.wait_recv()
 
@@ -281,10 +273,11 @@
 
     def prepare(g):
         rows = pl.ds(pl.multiple_of(g * group, LANES), group)
-        pot = pots[pl.ds(pl.multiple_of(g * 16 * ncol, 16), 16 * ncol), :].astype(jnp.float32)
         f, gp, w = [
             jnp.dot(
-                on_diagonal([pot[16 * b + k : 16 * b + k + 1, :] for b in range(ncol)]).astype(jnp.bfloat16),
+                on_diagonal(
+                    [pots[g * ncol + b, :, pl.ds(k * LANES, LANES)] for b in range(ncol)]
+                ).astype(jnp.bfloat16),
                 ones,
                 preferred_element_type=jnp.float32,
             )
@@ -361,11 +354,17 @@
         copy(slot, slot, hs.at[k], hr_sem.at[k], *peers[k]) for k in range(len(peers))
     ]
 
+    zg = send_z(gy_all, gy_ref, 1)
+    plane_g = [send_plane(gy_all, gy_ref, 1, 0)]
+
     def late(i, carry):
         build(near(jnp.minimum(i, 3)), near(jnp.minimum(6 - i, 3)))
         return carry
 
     lax.fori_loop(0, 7, late, 0)
+    p_own = jnp.exp(cross_own + (a_col[mine, :][:, :1] + b_lane[...]))
+    w_all = w_lane[...]
+    w_sum = jnp.sum(w_all, axis=1, keepdims=True)
     for c in sum_copies:
         c.wait_recv()
     for k in range(1, ncol):
@@ -431,10 +430,6 @@
     psi_own = psi_col[mine, :][:, :1]
     q_t = pt_own * (ht_own + (psi_own + phi))
     mix = jnp.dot(q_t.astype(jnp.bfloat16), x_all[...], preferred_element_type=jnp.float32)
-    p_own = jnp.exp(cross_own + (a_col[mine, :][:, :1] + b_lane[...]))
-
-    w_all = w_lane[...]
-    w_sum = jnp.sum(w_all, axis=1, keepdims=True)
     w_phi = jnp.sum(w_all * phi, axis=1, keepdims=True)
     phi_row = jnp.sum(jnp.where(eye, phi_own, 0.0), axis=0, keepdims=True)
     gw_ref[...] = (-(total / w_sum) * (phi_row - w_phi / w_sum))[:, :own]
@@ -464,9 +459,9 @@
     blocks = 4 * ncol
     total = own * blocks
     pot = jnp.pad(
-        jnp.stack([row_potential, col_potential, weights]), ((0, 13), (0, width - own))
-    )
-    pack = jnp.concatenate([particles, cotangent, pot], axis=0)
+        jnp.stack([row_potential, col_potential, weights]).astype(jnp.float32), ((0, 0), (0, LANES - own))
+    ).reshape(1, 3 * LANES)
+    pack = jnp.concatenate([particles, cotangent], axis=0)
     column = pltpu.VMEM((total, LANES), jnp.float32)
     line = pltpu.VMEM((1, total), jnp.float32)
     dma = pltpu.SemaphoreType.DMA
@@ -477,12 +472,12 @@
             jax.ShapeDtypeStruct((own, width), jnp.bfloat16),
             jax.ShapeDtypeStruct((1, own), jnp.float32),
         ),
-        in_specs=[vmem],
+        in_specs=[vmem, vmem],
         out_specs=[vmem, vmem],
         scratch_shapes=[
             pltpu.VMEM((total, width), jnp.bfloat16),
             pltpu.VMEM((total, width), jnp.bfloat16),
-            pltpu.VMEM((16 * blocks, LANES), jnp.bfloat16),
+            pltpu.VMEM((blocks, 1, 3 * LANES), jnp.float32),
             pltpu.VMEM((total, total), jnp.float32),
             column, column, column, column, column,
             line, line, line,
@@ -500,7 +495,7 @@
         cost_estimate=pl.CostEstimate(
             flops=3 * total * total * width, bytes_accessed=4 * own * width, transcendentals=total * total
         ),
-    )(pack)
+    )(pack, pot)
     return gp, gw.reshape(own)
 
 

time: 38.9 us -> 38.9 us (level)
    unnamed x8 -> x9, local copies, waits for them, and re-layouts: 1.8 us -> 1.8 us
where the time goes in v6:
time: 38.9 us; the launch traced here: 38.7 us
  Pallas kernels  35.4 us (91%)
  local copies, waits for them, and re-layouts  1.8 us (5%)
  other arithmetic  0.84 us (2%)
  between operations  0.67 us (2%)
    pallas_call x1, Pallas kernels, local_fused(): pl.pallas_call(functools.partial(fused_kernel, ncol, own), out_shape=(jax...  35.4 us
    unnamed x9, local copies, waits for them, and re-layouts  1.8 us
    concatenate x1, other arithmetic, local_fused(): pack = jnp.concatenate([particles, cotangent], axis=0)  0.83 us

profile of v6, /device:TPU:0, one launch (start us, length us, event | category | flops | bytes accessed | tf_op | source)
XLA Modules:
  0.0 38.7 jit_solution(4261949547149719605)
XLA Ops:
  0.6 0.0 copy-start
  0.6 0.0 copy-start.1
  0.7 0.0 copy-start.2
  0.7 0.6 %copy-done = bf16[96]{0:T(256)(128)(2,1)S(1)} copy-done((bf16[96]{0:T(256)(128)(2,1)S(1)}, bf16[96]{0:T(256)(128)(2,1)}, u32[]{:S(2)}) %copy-start) | copy-done | bytes 216
  1.3 0.0 copy-done.1
  1.3 0.0 copy-done.2
  1.3 0.8 %pad_maximum_fusion.pack_ref = bf16[192,256]{1,0:T(8,128)(2,1)S(1)} fusion(bf16[96,256]{1,0:T(8,128)(2,1)} %param.6, bf16[96,256]{1,0:T(8,128)(2,1)} %param.5), kind=kLoop, calls=%fused_computation | loop fusion | flops 196608 | bytes 196608 | tf_op jit(solution)/shard_map/concatenate | solution.py:464
  2.2 35.4 %shard_map.68 = (bf16[96,256]{1,0:T(8,128)(2,1)S(1)}, f32[1,96]{1,0:T(1,128)S(1)}) custom-call(bf16[192,256]{1,0:T(8,128)(2,1)S(1)} %pad_maximum_fusion.pack_ref, f32[1,384]{1,0:T(1,128)S(1)} %bitcast.10), custom_call_target="tpu_custom_call" | custom-call | flops 1811939328 | bytes 98304 | tf_op jit(solution)/shard_map/pallas_call | solution.py:469
  37.6 0.6 %copy.12 = bf16[96,256]{1,0:T(8,128)(2,1)} copy(bf16[96,256]{1,0:T(8,128)(2,1)S(1)} %get-tuple-element.8) | data formatting | bytes 98304
  38.2 0.5 %copy.13 = f32[96]{0:T(128)} copy(f32[96]{0:T(128)S(1)} %bitcast.11) | data formatting | bytes 768
  (2 shorter events, 0.0 us)
Async XLA Ops:
  0.6 0.7 %copy-start = (bf16[96]{0:T(256)(128)(2,1)S(1)}, bf16[96]{0:T(256)(128)(2,1)}, u32[]{:S(2)}) copy-start(bf16[96]{0:T(256)(128)(2,1)} %param.9) | copy-start | bytes 580
  0.6 0.7 %copy-start.1 = (bf16[96]{0:T(256)(128)(2,1)S(1)}, bf16[96]{0:T(256)(128)(2,1)}, u32[]{:S(2)}) copy-start(bf16[96]{0:T(256)(128)(2,1)} %param.8) | copy-start | bytes 580
  0.7 0.7 %copy-start.2 = (bf16[96]{0:T(256)(128)(2,1)S(1)}, bf16[96]{0:T(256)(128)(2,1)}, u32[]{:S(2)}) copy-start(bf16[96]{0:T(256)(128)(2,1)} %param.7) | copy-start | bytes 580

commit v7 on v6

--- a/solution.py
+++ b/solution.py
@@ -150,7 +150,7 @@
 def fused_kernel(
     ncol, own, pack_ref, pot_ref, gp_ref, gw_ref,
     x_all, gy_all, pots, plan, a_col, b_col, c_col, nhc_col, psi_col,
-    a_lane, b_lane, w_lane, r_acc, sums_all,
+    a_lane, b_lane, w_lane, r_acc, sums_all, p_own, pt_own, ht_own,
     ls, zs, zr, xs, xr, ps, pr, hs, hr_sem,
 ):
     nrow = 4
@@ -249,6 +249,7 @@
         zx[k - 1].wait_recv()
         plane_x.append(send_plane(x_all, x_ref, 0, k))
     zx += relay(x_all, 0, plane_x[0][2])
+    zg = send_z(gy_all, gy_ref, 1)
     for c in pot_copies:
         c.wait_recv()
 
@@ -334,27 +335,40 @@
         return carry
 
     lax.fori_loop(1, 9, early, 0)
+    x_own = x_ref[...]
+    gy_own = gy_ref[...]
+    slot = sums_all.at[me]
+
+    def own_terms(g):
+        rows = pl.ds(pl.multiple_of(g * group, LANES), group)
+        cross = nt(x_own, x_all[rows, :]) * scale
+        a = a_col[mine, :][:, :1]
+        b = b_col[mine, :][:, :1]
+        p_own[:, rows] = jnp.exp(cross + (a + b_lane[0:1, rows]))
+        p_t = jnp.exp(cross + (b + a_lane[0:1, rows]))
+        h_t = nt(gy_own, x_all[rows, :])
+        pt_own[:, rows] = p_t
+        ht_own[:, rows] = h_t
+        ph = p_t * h_t
+        slot[:, rows] = jnp.sum(fold(ph), axis=0, keepdims=True)
+        part = ph[:, :LANES]
+        for t in range(1, group // LANES):
+            part = part + ph[:, t * LANES : (t + 1) * LANES]
+        return part
+
+    hc_part = lax.fori_loop(
+        0, 3, lambda i, part: part + own_terms(near(i)), jnp.zeros((own, LANES), jnp.float32)
+    )
     for sent in plane_x[1:]:
         sent[2].wait_recv()
     for c in zx[ncol - 1 :]:
         c.wait_recv()
     prepare(dn)
-
-    x_own = x_all[mine, :]
-    local_g.wait()
-    cross_own = nt(x_own, x_all[...]) * scale
-    pt_own = jnp.exp(cross_own + (b_col[mine, :][:, :1] + a_lane[...]))
-    ht_own = nt(gy_all[mine, :], x_all[...])
-    ph = pt_own * ht_own
-    hc_own = jnp.sum(ph, axis=1, keepdims=True)
-    slot = sums_all.at[me]
-    slot[:, pl.ds(0, total)] = jnp.sum(fold(ph), axis=0, keepdims=True)
+    hc_own = lane_sums(hc_part + own_terms(dn))
     slot[:, pl.ds(total, LANES)] = jnp.sum(jnp.where(eye, hc_own, 0.0), axis=0, keepdims=True)
     sum_copies = [
         copy(slot, slot, hs.at[k], hr_sem.at[k], *peers[k]) for k in range(len(peers))
     ]
-
-    zg = send_z(gy_all, gy_ref, 1)
     plane_g = [send_plane(gy_all, gy_ref, 1, 0)]
 
     def late(i, carry):
@@ -362,15 +376,15 @@
         return carry
 
     lax.fori_loop(0, 7, late, 0)
-    p_own = jnp.exp(cross_own + (a_col[mine, :][:, :1] + b_lane[...]))
+    local_g.wait()
+    for k in range(1, ncol):
+        zg[k - 1].wait_recv()
+        plane_g.append(send_plane(gy_all, gy_ref, 1, k))
+    zg += relay(gy_all, 1, plane_g[0][2])
     w_all = w_lane[...]
     w_sum = jnp.sum(w_all, axis=1, keepdims=True)
     for c in sum_copies:
         c.wait_recv()
-    for k in range(1, ncol):
-        zg[k - 1].wait_recv()
-        plane_g.append(send_plane(gy_all, gy_ref, 1, k))
-    zg += relay(gy_all, 1, plane_g[0][2])
 
     for g in range(nrow):
         rows = pl.ds(g * group, group)
@@ -428,7 +442,7 @@
     )
     phi_own = jnp.sum(jnp.where(pick, phi, 0.0), axis=1, keepdims=True)
     psi_own = psi_col[mine, :][:, :1]
-    q_t = pt_own * (ht_own + (psi_own + phi))
+    q_t = pt_own[...] * (ht_own[...] + (psi_own + phi))
     mix = jnp.dot(q_t.astype(jnp.bfloat16), x_all[...], preferred_element_type=jnp.float32)
     w_phi = jnp.sum(w_all * phi, axis=1, keepdims=True)
     phi_row = jnp.sum(jnp.where(eye, phi_own, 0.0), axis=0, keepdims=True)
@@ -441,9 +455,9 @@
             plane_g[k][2].wait_recv()
     for c in zg[ncol - 1 :]:
         c.wait_recv()
-    q_own = p_own * (nt(x_own, gy_all[...]) + (phi_own + psi_lane))
+    q_own = p_own[...] * (nt(x_own, gy_all[...]) + (phi_own + psi_lane))
     q_sum = jnp.sum(q_own, axis=1, keepdims=True)
-    rowterm = jnp.dot(p_own.astype(jnp.bfloat16), gy_all[...], preferred_element_type=jnp.float32)
+    rowterm = jnp.dot(p_own[...].astype(jnp.bfloat16), gy_all[...], preferred_element_type=jnp.float32)
     mix = mix + jnp.dot(q_own.astype(jnp.bfloat16), x_all[...], preferred_element_type=jnp.float32)
     gp_ref[...] = (rowterm + (mix - q_sum * x_own.astype(jnp.float32)) * scale).astype(jnp.bfloat16)
 
@@ -463,6 +477,7 @@
     ).reshape(1, 3 * LANES)
     pack = jnp.concatenate([particles, cotangent], axis=0)
     column = pltpu.VMEM((total, LANES), jnp.float32)
+    strip = pltpu.VMEM((own, total), jnp.float32)
     line = pltpu.VMEM((1, total), jnp.float32)
     dma = pltpu.SemaphoreType.DMA
     vmem = pl.BlockSpec(memory_space=pltpu.VMEM)
@@ -483,6 +498,7 @@
             line, line, line,
             pltpu.VMEM((SUBL, total), jnp.float32),
             pltpu.VMEM((blocks, 1, total + LANES), jnp.float32),
+            strip, strip, strip,
             dma((2,)),
             dma((4 * (ncol - 1),)), dma((4 * (ncol - 1),)),
             dma((6 * ncol,)), dma((6 * ncol,)),

time: 38.9 us -> 38.5 us (0.990)
  Pallas kernels: 35.4 us -> 35 us
where the time goes in v7:
time: 38.5 us; the launch traced here: 38.3 us
  Pallas kernels  35 us (91%)
  local copies, waits for them, and re-layouts  1.8 us (5%)
  other arithmetic  0.84 us (2%)
  between operations  0.67 us (2%)
    pallas_call x1, Pallas kernels, local_fused(): pl.pallas_call(functools.partial(fused_kernel, ncol, own), out_shape=(jax...  35 us
    unnamed x9, local copies, waits for them, and re-layouts  1.8 us
    concatenate x1, other arithmetic, local_fused(): pack = jnp.concatenate([particles, cotangent], axis=0)  0.83 us

profile of v7, /device:TPU:0, one launch (start us, length us, event | category | flops | bytes accessed | tf_op | source)
XLA Modules:
  0.0 38.3 jit_solution(15683606610351093666)
XLA Ops:
  0.6 0.0 copy-start
  0.6 0.0 copy-start.1
  0.7 0.0 copy-start.2
  0.7 0.6 %copy-done = bf16[96]{0:T(256)(128)(2,1)S(1)} copy-done((bf16[96]{0:T(256)(128)(2,1)S(1)}, bf16[96]{0:T(256)(128)(2,1)}, u32[]{:S(2)}) %copy-start) | copy-done | bytes 216
  1.3 0.0 copy-done.1
  1.3 0.0 copy-done.2
  1.3 0.8 %pad_maximum_fusion.pack_ref = bf16[192,256]{1,0:T(8,128)(2,1)S(1)} fusion(bf16[96,256]{1,0:T(8,128)(2,1)} %param.6, bf16[96,256]{1,0:T(8,128)(2,1)} %param.5), kind=kLoop, calls=%fused_computation | loop fusion | flops 196608 | bytes 196608 | tf_op jit(solution)/shard_map/concatenate | solution.py:478
  2.2 35.0 %shard_map.68 = (bf16[96,256]{1,0:T(8,128)(2,1)S(1)}, f32[1,96]{1,0:T(1,128)S(1)}) custom-call(bf16[192,256]{1,0:T(8,128)(2,1)S(1)} %pad_maximum_fusion.pack_ref, f32[1,384]{1,0:T(1,128)S(1)} %bitcast.10), custom_call_target="tpu_custom_call" | custom-call | flops 1811939328 | bytes 98304 | tf_op jit(solution)/shard_map/pallas_call | solution.py:484
  37.2 0.6 %copy.12 = bf16[96,256]{1,0:T(8,128)(2,1)} copy(bf16[96,256]{1,0:T(8,128)(2,1)S(1)} %get-tuple-element.8) | data formatting | bytes 98304
  37.8 0.5 %copy.13 = f32[96]{0:T(128)} copy(f32[96]{0:T(128)S(1)} %bitcast.11) | data formatting | bytes 768
  (2 shorter events, 0.0 us)
Async XLA Ops:
  0.6 0.7 %copy-start = (bf16[96]{0:T(256)(128)(2,1)S(1)}, bf16[96]{0:T(256)(128)(2,1)}, u32[]{:S(2)}) copy-start(bf16[96]{0:T(256)(128)(2,1)} %param.9) | copy-start | bytes 580
  0.6 0.7 %copy-start.1 = (bf16[96]{0:T(256)(128)(2,1)S(1)}, bf16[96]{0:T(256)(128)(2,1)}, u32[]{:S(2)}) copy-start(bf16[96]{0:T(256)(128)(2,1)} %param.8) | copy-start | bytes 580
  0.7 0.7 %copy-start.2 = (bf16[96]{0:T(256)(128)(2,1)S(1)}, bf16[96]{0:T(256)(128)(2,1)}, u32[]{:S(2)}) copy-start(bf16[96]{0:T(256)(128)(2,1)} %param.7) | copy-start | bytes 580

commit v8 on v7

--- a/solution.py
+++ b/solution.py
@@ -325,10 +325,13 @@
     build(me_r, me_r)
     for sent in plane_x:
         sent[0].wait_recv()
-    prepare(xn)
-    for sent in plane_x:
         sent[1].wait_recv()
-    prepare(yn)
+
+    def prepare_near(u, carry):
+        prepare(near(u))
+        return carry
+
+    lax.fori_loop(1, 3, prepare_near, 0)
 
     def early(i, carry):
         build(near(i // 3), near(i % 3))
@@ -369,7 +372,6 @@
     sum_copies = [
         copy(slot, slot, hs.at[k], hr_sem.at[k], *peers[k]) for k in range(len(peers))
     ]
-    plane_g = [send_plane(gy_all, gy_ref, 1, 0)]
 
     def late(i, carry):
         build(near(jnp.minimum(i, 3)), near(jnp.minimum(6 - i, 3)))
@@ -377,6 +379,7 @@
 
     lax.fori_loop(0, 7, late, 0)
     local_g.wait()
+    plane_g = [send_plane(gy_all, gy_ref, 1, 0)]
     for k in range(1, ncol):
         zg[k - 1].wait_recv()
         plane_g.append(send_plane(gy_all, gy_ref, 1, k))
@@ -386,12 +389,15 @@
     for c in sum_copies:
         c.wait_recv()
 
-    for g in range(nrow):
-        rows = pl.ds(g * group, group)
+    def masses(g, carry):
+        rows = pl.ds(pl.multiple_of(g * group, LANES), group)
         inv = 1.0 / lane_sums(c_col[rows, :])
         c_col[rows, :] = inv
         lines = [sums_all[g * ncol + b, :, pl.ds(total, LANES)] for b in range(ncol)]
         nhc_col[rows, :] = -lane_sums(on_diagonal(lines)) * inv
+        return carry
+
+    lax.fori_loop(0, nrow, masses, 0)
     hr = jnp.sum(sums_all[:, :, pl.ds(0, total)], axis=0)
     inv_r = 1.0 / jnp.sum(r_acc[...], axis=0, keepdims=True)
     phi = -hr * inv_r
@@ -432,8 +438,12 @@
         return -(hr + jnp.sum(jnp.concatenate(accs, axis=1), axis=0, keepdims=True)) * inv_r
 
     phi = lax.fori_loop(1, ITERS, sweep, phi)
-    for g in range(nrow):
-        psi_col[pl.ds(g * group, group), :] = psi_of(g, phi)
+
+    def last(g, carry):
+        psi_col[pl.ds(pl.multiple_of(g * group, LANES), group), :] = psi_of(g, phi)
+        return carry
+
+    lax.fori_loop(0, nrow, last, 0)
     psi_lane = jnp.concatenate(
         [to_lanes(psi_col[pl.ds(t * LANES, LANES), :]) for t in range(tiles)], axis=1
     )

time: 38.5 us -> 41.6 us (1.081)
  Pallas kernels: 35 us -> 38.1 us
    pallas_call x1, Pallas kernels: 35 us -> 38.1 us  [local_fused(): pl.pallas_call(functools.partial(fused_kernel, ncol, own), out_shape=(jax...]
where the time goes in v8:
time: 41.6 us; the launch traced here: 41.4 us
  Pallas kernels  38.1 us (92%)
  local copies, waits for them, and re-layouts  1.8 us (4%)
  other arithmetic  0.84 us (2%)
  between operations  0.67 us (2%)
    pallas_call x1, Pallas kernels, local_fused(): pl.pallas_call(functools.partial(fused_kernel, ncol, own), out_shape=(jax...  38.1 us
    unnamed x9, local copies, waits for them, and re-layouts  1.8 us
    concatenate x1, other arithmetic, local_fused(): pack = jnp.concatenate([particles, cotangent], axis=0)  0.83 us

profile of v8, /device:TPU:0, one launch (start us, length us, event | category | flops | bytes accessed | tf_op | source)
XLA Modules:
  0.0 41.4 jit_solution(15164284961998806330)
XLA Ops:
  0.6 0.0 copy-start
  0.6 0.0 copy-start.1
  0.7 0.0 copy-start.2
  0.7 0.6 %copy-done = bf16[96]{0:T(256)(128)(2,1)S(1)} copy-done((bf16[96]{0:T(256)(128)(2,1)S(1)}, bf16[96]{0:T(256)(128)(2,1)}, u32[]{:S(2)}) %copy-start) | copy-done | bytes 216
  1.3 0.0 copy-done.1
  1.3 0.0 copy-done.2
  1.3 0.8 %pad_maximum_fusion.pack_ref = bf16[192,256]{1,0:T(8,128)(2,1)S(1)} fusion(bf16[96,256]{1,0:T(8,128)(2,1)} %param.6, bf16[96,256]{1,0:T(8,128)(2,1)} %param.5), kind=kLoop, calls=%fused_computation | loop fusion | flops 196608 | bytes 196608 | tf_op jit(solution)/shard_map/concatenate | solution.py:488
  2.2 38.1 %shard_map.68 = (bf16[96,256]{1,0:T(8,128)(2,1)S(1)}, f32[1,96]{1,0:T(1,128)S(1)}) custom-call(bf16[192,256]{1,0:T(8,128)(2,1)S(1)} %pad_maximum_fusion.pack_ref, f32[1,384]{1,0:T(1,128)S(1)} %bitcast.10), custom_call_target="tpu_custom_call" | custom-call | flops 1811939328 | bytes 98304 | tf_op jit(solution)/shard_map/pallas_call | solution.py:494
  40.3 0.6 %copy.12 = bf16[96,256]{1,0:T(8,128)(2,1)} copy(bf16[96,256]{1,0:T(8,128)(2,1)S(1)} %get-tuple-element.8) | data formatting | bytes 98304
  40.9 0.5 %copy.13 = f32[96]{0:T(128)} copy(f32[96]{0:T(128)S(1)} %bitcast.11) | data formatting | bytes 768
  (2 shorter events, 0.0 us)
Async XLA Ops:
  0.6 0.7 %copy-start = (bf16[96]{0:T(256)(128)(2,1)S(1)}, bf16[96]{0:T(256)(128)(2,1)}, u32[]{:S(2)}) copy-start(bf16[96]{0:T(256)(128)(2,1)} %param.9) | copy-start | bytes 580
  0.6 0.7 %copy-start.1 = (bf16[96]{0:T(256)(128)(2,1)S(1)}, bf16[96]{0:T(256)(128)(2,1)}, u32[]{:S(2)}) copy-start(bf16[96]{0:T(256)(128)(2,1)} %param.8) | copy-start | bytes 580
  0.7 0.7 %copy-start.2 = (bf16[96]{0:T(256)(128)(2,1)S(1)}, bf16[96]{0:T(256)(128)(2,1)}, u32[]{:S(2)}) copy-start(bf16[96]{0:T(256)(128)(2,1)} %param.7) | copy-start | bytes 580

commit v9 on v7

--- a/solution.py
+++ b/solution.py
@@ -250,6 +250,7 @@
         plane_x.append(send_plane(x_all, x_ref, 0, k))
     zx += relay(x_all, 0, plane_x[0][2])
     zg = send_z(gy_all, gy_ref, 1)
+    plane_g = [send_plane(gy_all, gy_ref, 1, 0)]
     for c in pot_copies:
         c.wait_recv()
 
@@ -369,18 +370,17 @@
     sum_copies = [
         copy(slot, slot, hs.at[k], hr_sem.at[k], *peers[k]) for k in range(len(peers))
     ]
-    plane_g = [send_plane(gy_all, gy_ref, 1, 0)]
-
-    def late(i, carry):
-        build(near(jnp.minimum(i, 3)), near(jnp.minimum(6 - i, 3)))
-        return carry
-
-    lax.fori_loop(0, 7, late, 0)
-    local_g.wait()
     for k in range(1, ncol):
         zg[k - 1].wait_recv()
         plane_g.append(send_plane(gy_all, gy_ref, 1, k))
     zg += relay(gy_all, 1, plane_g[0][2])
+
+    def late(i, carry):
+        build(near(jnp.minimum(i, 3)), near(jnp.minimum(6 - i, 3)))
+        return carry
+
+    lax.fori_loop(0, 7, late, 0)
+    local_g.wait()
     w_all = w_lane[...]
     w_sum = jnp.sum(w_all, axis=1, keepdims=True)
     for c in sum_copies:

time: 38.5 us -> 38.5 us (level)
  no operation moved by 1% of the time
where the time goes in v9:
time: 38.5 us; the launch traced here: 38.3 us
  Pallas kernels  35 us (91%)
  local copies, waits for them, and re-layouts  1.8 us (5%)
  other arithmetic  0.84 us (2%)
  between operations  0.67 us (2%)
    pallas_call x1, Pallas kernels, local_fused(): pl.pallas_call(functools.partial(fused_kernel, ncol, own), out_shape=(jax...  35 us
    unnamed x9, local copies, waits for them, and re-layouts  1.8 us
    concatenate x1, other arithmetic, local_fused(): pack = jnp.concatenate([particles, cotangent], axis=0)  0.83 us

profile of v9, /device:TPU:0, one launch (start us, length us, event | category | flops | bytes accessed | tf_op | source)
XLA Modules:
  0.0 38.3 jit_solution(13702429017307603923)
XLA Ops:
  0.6 0.0 copy-start
  0.6 0.0 copy-start.1
  0.7 0.0 copy-start.2
  0.7 0.6 %copy-done = bf16[96]{0:T(256)(128)(2,1)S(1)} copy-done((bf16[96]{0:T(256)(128)(2,1)S(1)}, bf16[96]{0:T(256)(128)(2,1)}, u32[]{:S(2)}) %copy-start) | copy-done | bytes 216
  1.3 0.0 copy-done.1
  1.3 0.0 copy-done.2
  1.3 0.8 %pad_maximum_fusion.pack_ref = bf16[192,256]{1,0:T(8,128)(2,1)S(1)} fusion(bf16[96,256]{1,0:T(8,128)(2,1)} %param.6, bf16[96,256]{1,0:T(8,128)(2,1)} %param.5), kind=kLoop, calls=%fused_computation | loop fusion | flops 196608 | bytes 196608 | tf_op jit(solution)/shard_map/concatenate | solution.py:478
  2.2 35.0 %shard_map.68 = (bf16[96,256]{1,0:T(8,128)(2,1)S(1)}, f32[1,96]{1,0:T(1,128)S(1)}) custom-call(bf16[192,256]{1,0:T(8,128)(2,1)S(1)} %pad_maximum_fusion.pack_ref, f32[1,384]{1,0:T(1,128)S(1)} %bitcast.10), custom_call_target="tpu_custom_call" | custom-call | flops 1811939328 | bytes 98304 | tf_op jit(solution)/shard_map/pallas_call | solution.py:484
  37.2 0.6 %copy.12 = bf16[96,256]{1,0:T(8,128)(2,1)} copy(bf16[96,256]{1,0:T(8,128)(2,1)S(1)} %get-tuple-element.8) | data formatting | bytes 98304
  37.8 0.5 %copy.13 = f32[96]{0:T(128)} copy(f32[96]{0:T(128)S(1)} %bitcast.11) | data formatting | bytes 768
  (2 shorter events, 0.0 us)
Async XLA Ops:
  0.6 0.7 %copy-start = (bf16[96]{0:T(256)(128)(2,1)S(1)}, bf16[96]{0:T(256)(128)(2,1)}, u32[]{:S(2)}) copy-start(bf16[96]{0:T(256)(128)(2,1)} %param.9) | copy-start | bytes 580
  0.6 0.7 %copy-start.1 = (bf16[96]{0:T(256)(128)(2,1)S(1)}, bf16[96]{0:T(256)(128)(2,1)}, u32[]{:S(2)}) copy-start(bf16[96]{0:T(256)(128)(2,1)} %param.8) | copy-start | bytes 580
  0.7 0.7 %copy-start.2 = (bf16[96]{0:T(256)(128)(2,1)S(1)}, bf16[96]{0:T(256)(128)(2,1)}, u32[]{:S(2)}) copy-start(bf16[96]{0:T(256)(128)(2,1)} %param.7) | copy-start | bytes 580
